TPU v7x, 32 devices: a whole 2x2x4 slice. The times are simulated.
32 devices in a mesh: shard: 8 (over z, y), rep: 4 (over x, core).
Axes of the slice: x: 2, y: 2, z: 4, core: 2. Of those that a mesh axis runs over, the one named last changes fastest.
Arguments:
- tokens: bfloat16 [32768, 768], P(('shard', 'rep')), may hold values from -6 to 6
- lengths: int32 [32], P(('shard', 'rep')), may hold values from 1 to 1024, 24576 in all
- expert_choice: int32 [32768, 1], P(('shard', 'rep')), may hold values from 0 to 7
- query_weight: bfloat16 [768, 768], P('shard'), may hold values from -0.21875 to 0.21875
- key_weight: bfloat16 [768, 768], P('shard'), may hold values from -0.21875 to 0.21875
- value_weight: bfloat16 [768, 768], P('shard'), may hold values from -0.21875 to 0.21875
- output_weight: bfloat16 [768, 768], P('shard'), may hold values from -3.5 to 3.5
- first_gain: bfloat16 [768], P('shard'), may hold values from 0.5 to 1.5
- second_gain: bfloat16 [768], P('shard'), may hold values from 0.5 to 1.5
- router_weight: bfloat16 [768, 8], P('shard'), may hold values from -0.15625 to 0.15625
- bias_table: bfloat16 [32, 12], P('shard'), may hold values from -4 to 4
- expert_in: bfloat16 [8, 768, 3072], P('shard'), may hold values from -0.21875 to 0.21875
- expert_out: bfloat16 [8, 3072, 768], P('shard'), may hold values from -0.875 to 0.875
- cotangent: bfloat16 [32768, 768], P(('shard', 'rep')), may hold values from -6 to 6
Outputs:
- layer_out: bfloat16 [32768, 768], P(('shard', 'rep'))
- token_grad: bfloat16 [32768, 768], P(('shard', 'rep'))
- query_weight_grad: float32 [768, 768], P('shard')
- key_weight_grad: float32 [768, 768], P('shard')
- value_weight_grad: float32 [768, 768], P('shard')
- output_weight_grad: float32 [768, 768], P('shard')
- first_gain_grad: float32 [768], P('shard')
- second_gain_grad: float32 [768], P('shard')
- router_weight_grad: float32 [768, 8], P('shard')
- bias_table_grad: float32 [32, 12], P('shard')
- expert_in_grad: float32 [8, 768, 3072], P('shard')
- expert_out_grad: float32 [8, 3072, 768], P('shard')
Inputs may be any that keep to these rules, and one draw needn't show every extreme that they name: `lengths`: some sequence is 1024 tokens long. `expert_choice`: every expert is chosen by some token.
All inputs are finite; a program needn't handle non-finite values. No bound on the sum of `lengths` on one device may be relied on, other than what follows from the above.
Results may differ from a plain program's by a relative error of at most 0.02.
Values may be sent and summed in bfloat16 or wider, within the bound.
A program may use at most 320 MiB of HBM per device.

v0:
```python
import jax
import jax.numpy as jnp
import numpy as np
from jax import lax
from jax.sharding import PartitionSpec as P

MAX_DISTANCE = 128


EPSILON = 1e-06
MASKED = -1000000000.0


def bucket_levels(slot_count, bucket_count, reach):
    half_count = bucket_count // 2
    exact_count = half_count // 2
    distance = np.arange(slot_count)
    spread_log = (
        np.log(np.maximum(distance, 1) / exact_count)
        / np.log(reach / exact_count)
        * (half_count - exact_count)
    )
    far_bucket = np.minimum(
        exact_count + np.maximum(spread_log, 0.0).astype(np.int64), half_count - 1
    )
    far_bucket = np.where(distance < exact_count, exact_count, far_bucket)
    levels = []
    for level in range(exact_count + 1, half_count):
        reached = far_bucket >= level
        if np.any(reached):
            levels.append(int(np.argmax(reached)))
    return (half_count, exact_count, levels)


def block_onehot(first_row, block_rows, slot_count, bucket_count, reach):
    half_count, exact_count, levels = bucket_levels(slot_count, bucket_count, reach)
    rows_here = first_row + jnp.arange(block_rows, dtype=jnp.int32)[:, None]
    columns = jnp.arange(slot_count, dtype=jnp.int32)[None, :]
    offset_value = columns - rows_here
    distance = jnp.abs(offset_value)
    far_bucket = jnp.full(distance.shape, exact_count, jnp.int32)
    for threshold in levels:
        far_bucket = far_bucket + (distance >= threshold).astype(jnp.int32)
    bucket_ids = jnp.where(offset_value > 0, half_count, 0) + jnp.where(
        distance < exact_count, distance, far_bucket
    )
    return (
        bucket_ids[:, :, None] == jnp.arange(bucket_count, dtype=jnp.int32)[None, None, :]
    ).astype(jnp.bfloat16)


def contract(left_side, right_side, left_axis, right_axis):
    return lax.dot_general(
        left_side,
        right_side,
        (((left_axis,), (right_axis,)), ((), ())),
        preferred_element_type=jnp.float32,
    )


def rms_forward(values, gain):
    inverse = lax.rsqrt(jnp.mean(values * values, axis=-1, keepdims=True) + EPSILON)
    return (values * inverse * gain, inverse)


def rms_backward(values, inverse, gain, upstream):
    scaled = upstream * gain
    gain_grad = jnp.sum(upstream * values * inverse, axis=0)
    inner_mean = jnp.mean(scaled * values, axis=-1, keepdims=True)
    return (inverse * scaled - values * inverse * inverse * inverse * inner_mean, gain_grad)


def on_device(
    tokens,
    lengths,
    expert_choice,
    query_weight,
    key_weight,
    value_weight,
    output_weight,
    first_gain,
    second_gain,
    router_weight,
    bias_table,
    expert_in,
    expert_out,
    cotangent,
):
    token_count, model_width = tokens.shape
    group_size = lax.axis_size("shard")
    head_count = bias_table.shape[1]
    head_size = model_width // head_count
    expert_count = router_weight.shape[1]
    capacity = token_count // group_size
    block_rows = min(512, token_count)
    bucket_count = bias_table.shape[0] * group_size
    block_starts = list(range(0, token_count, block_rows))
    live_mask = jnp.arange(token_count, dtype=jnp.int32) < lengths[0]
    gathered = (
        lax.all_gather(query_weight, "shard", axis=0, tiled=True),
        lax.all_gather(key_weight, "shard", axis=0, tiled=True),
        lax.all_gather(value_weight, "shard", axis=0, tiled=True),
        lax.all_gather(output_weight, "shard", axis=0, tiled=True),
        lax.all_gather(first_gain, "shard", axis=0, tiled=True),
        lax.all_gather(second_gain, "shard", axis=0, tiled=True),
        lax.all_gather(router_weight, "shard", axis=0, tiled=True),
        lax.all_gather(bias_table, "shard", axis=0, tiled=True),
    )
    full_query, full_key, full_value, full_output = (
        gathered[0],
        gathered[1],
        gathered[2],
        gathered[3],
    )
    first_scale = gathered[4].astype(jnp.float32)
    second_scale = gathered[5].astype(jnp.float32)
    full_router = gathered[6]
    table_low = gathered[7]
    inputs = tokens.astype(jnp.float32)
    normed, first_inverse = rms_forward(inputs, first_scale)
    normed_low = normed.astype(jnp.bfloat16)
    head_shape = (token_count, head_count, head_size)
    queries = (
        jnp.dot(normed_low, full_query, preferred_element_type=jnp.float32)
        .astype(jnp.bfloat16)
        .reshape(head_shape)
    )
    keys_low = (
        jnp.dot(normed_low, full_key, preferred_element_type=jnp.float32)
        .astype(jnp.bfloat16)
        .reshape(head_shape)
    )
    values_low = (
        jnp.dot(normed_low, full_value, preferred_element_type=jnp.float32)
        .astype(jnp.bfloat16)
        .reshape(head_shape)
    )

    def block_scores(first_row, onehot):
        scores = (
            jnp.einsum(
                "qhd,khd->hqk",
                queries[first_row : first_row + block_rows],
                keys_low,
                preferred_element_type=jnp.float32,
            )
            * 0.125
        )
        scores = scores + jnp.einsum(
            "qkc,ch->hqk", onehot, table_low, preferred_element_type=jnp.float32
        )
        return jnp.where(live_mask[None, None, :], scores, MASKED)

    attended_parts = []
    log_totals = []
    for first_row in block_starts:
        onehot = block_onehot(first_row, block_rows, token_count, bucket_count, MAX_DISTANCE)
        scores = block_scores(first_row, onehot)
        peak = jnp.max(scores, axis=-1, keepdims=True)
        weights = jnp.exp(scores - peak)
        total = jnp.sum(weights, axis=-1, keepdims=True)
        probs_low = (weights / total).astype(jnp.bfloat16)
        attended_parts.append(
            jnp.einsum("hqk,khd->qhd", probs_low, values_low, preferred_element_type=jnp.float32)
        )
        log_totals.append(peak + jnp.log(total))
    attended = (
        jnp.concatenate(attended_parts, axis=0)
        .reshape(token_count, model_width)
        .astype(jnp.bfloat16)
    )
    middle = inputs + jnp.dot(attended, full_output, preferred_element_type=jnp.float32)
    second, second_inverse = rms_forward(middle, second_scale)
    second_low = second.astype(jnp.bfloat16)
    logits = jnp.dot(second_low, full_router, preferred_element_type=jnp.float32)
    router_probs = jax.nn.softmax(logits, axis=-1)
    choice_hot = expert_choice == jnp.arange(expert_count, dtype=jnp.int32)[None, :]
    gates = jnp.sum(jnp.where(choice_hot, router_probs, 0.0), axis=1)
    hot_live = (choice_hot & live_mask[:, None]).astype(jnp.int32)
    before = jnp.cumsum(hot_live, axis=0) - hot_live
    slot = jnp.sum(before * hot_live, axis=1)
    kept = live_mask & (slot < capacity)
    target = jnp.where(kept, expert_choice[:, 0] * capacity + slot, -1)
    dispatch = (
        target[None, :] == jnp.arange(expert_count * capacity, dtype=jnp.int32)[:, None]
    ).astype(jnp.bfloat16)
    send_rows = jnp.dot(dispatch, second_low, preferred_element_type=jnp.float32).astype(
        jnp.bfloat16
    )
    send_rows = send_rows.reshape(expert_count, capacity, model_width)
    weight_in = expert_in[0]
    weight_out = expert_out[0]
    received = lax.all_to_all(send_rows, "shard", split_axis=0, concat_axis=0, tiled=True)
    flat_rows = received.reshape(-1, model_width)
    inner = jnp.dot(flat_rows, weight_in, preferred_element_type=jnp.float32)
    active = jax.nn.gelu(inner).astype(jnp.bfloat16)
    produced = jnp.dot(active, weight_out, preferred_element_type=jnp.float32).astype(jnp.bfloat16)
    returned = lax.all_to_all(
        produced.reshape(received.shape), "shard", split_axis=0, concat_axis=0, tiled=True
    )
    returned, inner_kept, received_kept = (
        returned,
        inner.reshape(received.shape[0], received.shape[1], -1),
        received,
    )
    combined = jnp.einsum(
        "st,sd->td",
        dispatch,
        returned.reshape(expert_count * capacity, model_width),
        preferred_element_type=jnp.float32,
    )
    layer_out = (middle + gates[:, None] * combined).astype(jnp.bfloat16)
    upstream = cotangent.astype(jnp.float32) * live_mask[:, None].astype(jnp.float32)
    gate_grad = jnp.sum(upstream * combined, axis=1)
    result_grad = (gates[:, None] * upstream).astype(jnp.bfloat16)
    send_grad = jnp.einsum(
        "st,td->sd", dispatch, result_grad, preferred_element_type=jnp.float32
    ).astype(jnp.bfloat16)
    arrived = lax.all_to_all(
        send_grad.reshape(expert_count, capacity, model_width),
        "shard",
        split_axis=0,
        concat_axis=0,
        tiled=True,
    )
    arrived_flat = arrived.reshape(-1, model_width)
    inner_flat = inner_kept.reshape(arrived_flat.shape[0], -1)
    active_value, active_pull = jax.vjp(jax.nn.gelu, inner_flat)
    active_low = active_value.astype(jnp.bfloat16)
    active_grad = contract(arrived_flat, weight_out, 1, 1)
    inner_grad = active_pull(active_grad)[0].astype(jnp.bfloat16)
    out_weight_grad = contract(active_low, arrived_flat, 0, 0)
    in_weight_grad = contract(received_kept.reshape(-1, model_width), inner_grad, 0, 0)
    rows_grad = contract(inner_grad, weight_in, 1, 1).astype(jnp.bfloat16).reshape(arrived.shape)
    rows_back = lax.all_to_all(rows_grad, "shard", split_axis=0, concat_axis=0, tiled=True)
    regathered = (
        lax.all_gather(query_weight, "shard", axis=0, tiled=True),
        lax.all_gather(key_weight, "shard", axis=0, tiled=True),
        lax.all_gather(value_weight, "shard", axis=0, tiled=True),
        lax.all_gather(output_weight, "shard", axis=0, tiled=True),
        lax.all_gather(router_weight, "shard", axis=0, tiled=True),
    )
    back_query, back_key, back_value, back_output, back_router = regathered
    chosen_float = choice_hot.astype(jnp.float32)
    logit_grad = (
        router_probs * (chosen_float * gate_grad[:, None] - (gates * gate_grad)[:, None])
    ).astype(jnp.bfloat16)
    router_grad = contract(second_low, logit_grad, 0, 0)
    second_grad = contract(logit_grad, back_router, 1, 1) + jnp.einsum(
        "st,sd->td",
        dispatch,
        rows_back.reshape(expert_count * capacity, model_width),
        preferred_element_type=jnp.float32,
    )
    middle_part, second_gain_grad = rms_backward(middle, second_inverse, second_scale, second_grad)
    middle_grad = upstream + middle_part
    branch_grad = middle_grad.astype(jnp.bfloat16)
    output_grad = contract(attended, branch_grad, 0, 0)
    attended_grad = (
        contract(branch_grad, back_output, 1, 1).astype(jnp.bfloat16).reshape(head_shape)
    )
    query_parts = []
    key_total = jnp.zeros(head_shape, jnp.float32)
    value_total = jnp.zeros(head_shape, jnp.float32)
    table_grad = jnp.zeros((bucket_count, head_count), jnp.float32)
    for block_number, first_row in enumerate(block_starts):
        onehot = block_onehot(first_row, block_rows, token_count, bucket_count, MAX_DISTANCE)
        scores = block_scores(first_row, onehot)
        probs_block = jnp.exp(scores - log_totals[block_number])
        probs_low = probs_block.astype(jnp.bfloat16)
        grad_block = attended_grad[first_row : first_row + block_rows]
        prob_grad = jnp.einsum(
            "qhd,khd->hqk", grad_block, values_low, preferred_element_type=jnp.float32
        )
        row_delta = jnp.sum(probs_block * prob_grad, axis=-1, keepdims=True)
        score_grad = (probs_block * (prob_grad - row_delta)).astype(jnp.bfloat16)
        value_total = value_total + jnp.einsum(
            "hqk,qhd->khd", probs_low, grad_block, preferred_element_type=jnp.float32
        )
        query_parts.append(
            jnp.einsum("hqk,khd->qhd", score_grad, keys_low, preferred_element_type=jnp.float32)
            * 0.125
        )
        key_total = (
            key_total
            + jnp.einsum(
                "hqk,qhd->khd",
                score_grad,
                queries[first_row : first_row + block_rows],
                preferred_element_type=jnp.float32,
            )
            * 0.125
        )
        table_grad = table_grad + jnp.einsum(
            "hqk,qkc->ch", score_grad, onehot, preferred_element_type=jnp.float32
        )
    query_low = (
        jnp.concatenate(query_parts, axis=0).reshape(token_count, model_width).astype(jnp.bfloat16)
    )
    key_low = key_total.reshape(token_count, model_width).astype(jnp.bfloat16)
    value_low = value_total.reshape(token_count, model_width).astype(jnp.bfloat16)
    query_grad = contract(normed_low, query_low, 0, 0)
    key_grad = contract(normed_low, key_low, 0, 0)
    value_grad = contract(normed_low, value_low, 0, 0)
    normed_grad = (
        contract(query_low, back_query, 1, 1)
        + contract(key_low, back_key, 1, 1)
        + contract(value_low, back_value, 1, 1)
    )
    input_part, first_gain_grad = rms_backward(inputs, first_inverse, first_scale, normed_grad)
    token_grad = (middle_grad + input_part).astype(jnp.bfloat16)
    group_sums = (
        lax.psum_scatter(
            query_grad.astype(jnp.bfloat16), "shard", scatter_dimension=0, tiled=True
        ).astype(jnp.float32),
        lax.psum_scatter(
            key_grad.astype(jnp.bfloat16), "shard", scatter_dimension=0, tiled=True
        ).astype(jnp.float32),
        lax.psum_scatter(
            value_grad.astype(jnp.bfloat16), "shard", scatter_dimension=0, tiled=True
        ).astype(jnp.float32),
        lax.psum_scatter(
            output_grad.astype(jnp.bfloat16), "shard", scatter_dimension=0, tiled=True
        ).astype(jnp.float32),
        lax.psum_scatter(
            first_gain_grad.astype(jnp.bfloat16), "shard", scatter_dimension=0, tiled=True
        ).astype(jnp.float32),
        lax.psum_scatter(
            second_gain_grad.astype(jnp.bfloat16), "shard", scatter_dimension=0, tiled=True
        ).astype(jnp.float32),
        lax.psum_scatter(
            router_grad.astype(jnp.bfloat16), "shard", scatter_dimension=0, tiled=True
        ).astype(jnp.float32),
        lax.psum_scatter(
            table_grad.astype(jnp.bfloat16), "shard", scatter_dimension=0, tiled=True
        ).astype(jnp.float32),
    )
    everything = (
        lax.psum(group_sums[0].astype(jnp.bfloat16), "rep").astype(jnp.float32),
        lax.psum(group_sums[1].astype(jnp.bfloat16), "rep").astype(jnp.float32),
        lax.psum(group_sums[2].astype(jnp.bfloat16), "rep").astype(jnp.float32),
        lax.psum(group_sums[3].astype(jnp.bfloat16), "rep").astype(jnp.float32),
        lax.psum(group_sums[4].astype(jnp.bfloat16), "rep").astype(jnp.float32),
        lax.psum(group_sums[5].astype(jnp.bfloat16), "rep").astype(jnp.float32),
        lax.psum(group_sums[6].astype(jnp.bfloat16), "rep").astype(jnp.float32),
        lax.psum(group_sums[7].astype(jnp.bfloat16), "rep").astype(jnp.float32),
        lax.psum(in_weight_grad.astype(jnp.bfloat16), "rep").astype(jnp.float32),
        lax.psum(out_weight_grad.astype(jnp.bfloat16), "rep").astype(jnp.float32),
    )
    replica_sums = everything[:8]
    in_total, out_total = (everything[8], everything[9])
    return (
        layer_out,
        token_grad,
        replica_sums[0],
        replica_sums[1],
        replica_sums[2],
        replica_sums[3],
        replica_sums[4],
        replica_sums[5],
        replica_sums[6],
        replica_sums[7],
        in_total[None],
        out_total[None],
    )


def solution(mesh):
    placed = (
        P(("shard", "rep"), None),
        P(("shard", "rep")),
        P(("shard", "rep"), None),
        P("shard", None),
        P("shard", None),
        P("shard", None),
        P("shard", None),
        P("shard"),
        P("shard"),
        P("shard", None),
        P("shard", None),
        P("shard", None, None),
        P("shard", None, None),
        P(("shard", "rep"), None),
    )
    return jax.shard_map(
        on_device,
        mesh=mesh,
        in_specs=placed,
        out_specs=(
            P(("shard", "rep"), None),
            P(("shard", "rep"), None),
            P("shard", None),
            P("shard", None),
            P("shard", None),
            P("shard", None),
            P("shard"),
            P("shard"),
            P("shard", None),
            P("shard", None),
            P("shard", None, None),
            P("shard", None, None),
        ),
        check_vma=False,
    )
```

profile of v0, /device:TPU:0, one launch (start us, length us, event | category | flops | bytes accessed | tf_op | source)
XLA Modules:
  0.0 978.9 jit_solution(1696143308467799473)
XLA Ops:
  16.2 23.1 %all-reduce.6 = (bf16[768]{0:T(1024)(128)(2,1)S(1)}, bf16[768]{0:T(1024)(128)(2,1)S(1)}) all-reduce(bf16[768]{0:T(1024)(128)(2,1)S(1)} %dynamic-update-slice, bf16[768]{0:T(1024)(128)(2,1)S(1)} %dynamic-update-slice.1), channel_id=1, replica_groups=mesh['shard'=8,'rep'=4] {'shard'}, use_global_device_ids=true, to_apply=%add | all-reduce | flops 1536 | bytes 6144
  40.0 16.6 %all-gather = bf16[8,4,12]{2,1,0:T(4,128)(2,1)S(1)} all-gather(bf16[1,4,12]{2,1,0:T(4,128)(2,1)} %bitcast.198), channel_id=1, replica_groups=mesh['shard'=8,'rep'=4] {'shard'}, dimensions={0}, use_global_device_ids=true | all-gather | bytes 864 | tf_op jit(solution)/shard_map/all_gather | solution.py:107
  61.2 3.4 fusion.58
  64.6 16.1 %fusion.3 = f32[512,1024,12]{0,2,1:T(8,128)} fusion(bf16[32,12,1]{1,0,2:T(8,128)(2,1)S(1)} %bitcast.194, s32[512,1024]{0,1:T(8,128)S(1)} %copy-done.9), kind=kOutput, calls=%fused_computation.5 | convolution fusion | flops 419430400 | bytes 27263744 | tf_op jit(solution)/shard_map/qkc,ch->hqk/dot_general | solution.py:149
  80.7 30.3 %copy.62 = f32[512,1024,12]{1,0,2:T(8,128)} copy(f32[512,1024,12]{0,2,1:T(8,128)} %fusion.3) | data formatting | bytes 50331648 | tf_op jit(solution)/shard_map/qkc,ch->hqk/dot_general | solution.py:149
  111.0 16.5 %fusion.1 = f32[512,1024,12]{0,2,1:T(8,128)} fusion(bf16[32,12,1]{1,0,2:T(8,128)(2,1)S(1)} %bitcast.195, s32[512,1024]{0,1:T(8,128)} %fusion.58), kind=kOutput, calls=%fused_computation.2 | convolution fusion | flops 419430400 | bytes 27263744 | tf_op jit(solution)/shard_map/qkc,ch->hqk/dot_general | solution.py:149
  127.5 30.5 %copy.64 = f32[512,1024,12]{1,0,2:T(8,128)} copy(f32[512,1024,12]{0,2,1:T(8,128)} %fusion.1) | data formatting | bytes 50331648 | tf_op jit(solution)/shard_map/qkc,ch->hqk/dot_general | solution.py:149
  158.1 2.8 convolution_convert_fusion.4
  162.2 2.8 convolution_convert_fusion.3
  165.0 16.3 %fusion.124 = (f32[12,512]{1,0:T(8,128)S(1)}, f32[12,512,1024]{2,1,0:T(8,128)}) fusion(f32[512,1024,12]{1,0,2:T(8,128)} %copy.62, bf16[512,12,64]{0,2,1:T(8,128)(2,1)} %bitcast.164, bf16[1024,12,64]{0,2,1:T(8,128)(2,1)S(1)} %bitcast.158, pred[1024]{0:T(1024)(128)(4,1)S(1)} %iota_compare_fusion.25), kind=kOutput, calls=%fused_computation.182 | convolution fusion | flops 830466048 | bytes 52716544 | tf_op jit(solution)/shard_map/qhd,khd->hqk/dot_general | solution.py:141
  181.3 10.9 %fusion.10 = f32[12,512]{1,0:T(8,128)S(1)} fusion(f32[12,512,1024]{2,1,0:T(8,128)} %get-tuple-element.78, f32[12,512]{1,0:T(8,128)S(1)} %get-tuple-element.77), kind=kLoop, calls=%fused_computation.24 | loop fusion | flops 12576768 | bytes 25214976 | tf_op jit(solution)/shard_map/reduce_sum | solution.py:161
  192.3 2.8 convolution_convert_fusion.5
  195.1 11.0 %fusion.97 = bf16[512,12,64]{0,2,1:T(8,128)(2,1)S(1)} fusion(bf16[1024,12,64]{0,2,1:T(8,128)(2,1)S(1)} %bitcast.170, f32[12,512,1024]{2,1,0:T(8,128)} %get-tuple-element.78, f32[12,512]{1,0:T(8,128)S(1)} %fusion.10, f32[12,512]{1,0:T(8,128)S(1)} %get-tuple-element.77), kind=kOutput, calls=%fused_computation.141 | convolution fusion | flops 824573952 | bytes 27574272 | tf_op jit(solution)/shard_map/hqk,khd->qhd/dot_general | solution.py:164
  206.1 16.2 %fusion.123 = (f32[12,512]{1,0:T(8,128)S(1)}, f32[12,512,1024]{2,1,0:T(8,128)}) fusion(f32[512,1024,12]{1,0,2:T(8,128)} %copy.64, bf16[512,12,64]{0,2,1:T(8,128)(2,1)S(1)} %bitcast.162, bf16[1024,12,64]{0,2,1:T(8,128)(2,1)S(1)} %bitcast.159, pred[1024]{0:T(1024)(128)(4,1)S(1)} %iota_compare_fusion.25), kind=kOutput, calls=%fused_computation.181 | convolution fusion | flops 830466048 | bytes 52716544 | tf_op jit(solution)/shard_map/qhd,khd->hqk/dot_general | solution.py:141
  222.2 11.0 %fusion.11 = f32[12,512]{1,0:T(8,128)S(1)} fusion(f32[12,512,1024]{2,1,0:T(8,128)} %get-tuple-element.76, f32[12,512]{1,0:T(8,128)S(1)} %get-tuple-element.75), kind=kLoop, calls=%fused_computation.25 | loop fusion | flops 12576768 | bytes 25214976 | tf_op jit(solution)/shard_map/reduce_sum | solution.py:161
  233.3 10.4 %fusion.98 = bf16[512,12,64]{0,2,1:T(8,128)(2,1)S(1)} fusion(bf16[1024,12,64]{0,2,1:T(8,128)(2,1)S(1)} %bitcast.172, f32[12,512,1024]{2,1,0:T(8,128)} %get-tuple-element.76, f32[12,512]{1,0:T(8,128)S(1)} %fusion.11, f32[12,512]{1,0:T(8,128)S(1)} %get-tuple-element.75), kind=kOutput, calls=%fused_computation.142 | convolution fusion | flops 824573952 | bytes 27574272 | tf_op jit(solution)/shard_map/hqk,khd->qhd/dot_general | solution.py:164
  245.1 3.8 multiply_reduce_fusion.5
  249.2 3.1 fusion.83
  252.4 4.4 all-to-all-start
  256.8 48.8 %all-gather.1 = bf16[8,96,8]{1,2,0:T(8,128)(2,1)S(1)} all-gather(bf16[1,96,8]{1,2,0:T(8,128)(2,1)S(1)} %bitcast.197), channel_id=1, replica_groups=mesh['shard'=8,'rep'=4] {'shard'}, dimensions={0}, use_global_device_ids=true | all-gather | bytes 13824 | tf_op jit(solution)/shard_map/all_gather | solution.py:106
  305.7 2.6 copy.66
  310.1 4.7 fusion.84
  314.8 4.5 all-to-all-start.2
  319.2 7.4 fusion.35
  326.6 4.6 copy-done.42
  331.2 10.8 %fusion.88 = bf16[1024,768]{1,0:T(8,128)(2,1)} fusion(bf16[1,3072,768]{2,1,0:T(8,128)(2,1)} %param.26, f32[1024,3072]{1,0:T(8,128)S(1)} %fusion.35), kind=kOutput, calls=%fused_computation.122 | convolution fusion | flops 4860936192 | bytes 18874368 | tf_op jit(solution)/shard_map/dot_general | solution.py:197
  342.0 7.9 all-to-all-done.2
  349.9 4.3 all-to-all-start.1
  354.2 15.4 %fusion.20 = bf16[1024,3072]{1,0:T(8,128)(2,1)S(1)} fusion(f32[1024,3072]{1,0:T(8,128)} %copy-done.42, bf16[1024,768]{1,0:T(8,128)(2,1)} %bitcast.26, bf16[1,3072,768]{2,1,0:T(8,128)(2,1)} %param.26), kind=kOutput, calls=%fused_computation.36 | convolution fusion | flops 4894752768 | bytes 25165824 | tf_op jit(solution)/shard_map/dot_general | solution.py:53
  369.6 2.7 copy-done.41
  372.3 8.5 fusion.85
  380.8 7.7 all-to-all-done.1
  388.5 4.3 all-to-all-start.3
  393.1 5.6 multiply_reduce_fusion.4
  398.7 30.5 %all-to-all-done.3 = bf16[8,128,768]{2,1,0:T(8,128)(2,1)} async-done(((bf16[8,128,768]{2,1,0:T(8,128)(2,1)}), bf16[8,128,768]{2,1,0:T(8,128)(2,1)}, u32[]{:S(2)}, u32[]{:S(2)}) %all-to-all-start.3) | async-done | bytes 1572896 | tf_op jit(solution)/shard_map/all_to_all | solution.py:235
  429.2 3.3 fusion.39
  434.9 2.8 subtract_add_fusion
  439.5 2.5 convolution_convert_fusion.6
  442.4 3.3 convolution_convert_fusion.2
  446.7 10.7 %fusion.21 = f32[12,64,1024]{2,1,0:T(8,128)S(1)} fusion(bf16[512,12,64]{0,2,1:T(8,128)(2,1)S(1)} %bitcast.166, f32[12,512,1024]{2,1,0:T(8,128)} %get-tuple-element.76, f32[12,512]{1,0:T(8,128)S(1)} %log_add_fusion), kind=kOutput, calls=%fused_computation.37 | convolution fusion | flops 817889280 | bytes 29122560 | tf_op jit(solution)/shard_map/hqk,qhd->khd/dot_general | solution.py:277
  457.4 16.7 %multiply_reduce_fusion.1 = (f32[12,512]{1,0:T(8,128)S(1)}, f32[12,512,1024]{2,1,0:T(8,128)}) fusion(f32[12,512,1024]{2,1,0:T(8,128)} %get-tuple-element.78, f32[12,512]{1,0:T(8,128)S(1)} %log_add_fusion.1, bf16[512,12,64]{0,2,1:T(8,128)(2,1)} %bitcast.168, bf16[1024,12,64]{0,2,1:T(8,128)(2,1)} %bitcast.171), kind=kOutput, calls=%fused_computation.18 | convolution fusion | flops 824174592 | bytes 52740096 | tf_op jit(solution)/shard_map/qhd,khd->hqk/dot_general | solution.py:272
  474.1 11.0 %add_convert_fusion = bf16[12,64,1024]{2,1,0:T(8,128)(2,1)S(1)} fusion(f32[12,64,1024]{2,1,0:T(8,128)S(1)} %fusion.21, bf16[512,12,64]{0,2,1:T(8,128)(2,1)} %bitcast.169, f32[12,512,1024]{2,1,0:T(8,128)} %get-tuple-element.78, f32[12,512]{1,0:T(8,128)S(1)} %log_add_fusion.1), kind=kOutput, calls=%fused_computation.81 | convolution fusion | flops 819462144 | bytes 30695424 | tf_op jit(solution)/shard_map/hqk,qhd->khd/dot_general | solution.py:277
  488.8 19.8 %multiply_reduce_fusion = (f32[12,512]{1,0:T(8,128)S(1)}, f32[12,512,1024]{2,1,0:T(8,128)}) fusion(f32[12,512,1024]{2,1,0:T(8,128)} %get-tuple-element.76, f32[12,512]{1,0:T(8,128)S(1)} %log_add_fusion, bf16[512,12,64]{0,2,1:T(8,128)(2,1)S(1)} %bitcast.167, bf16[1024,12,64]{0,2,1:T(8,128)(2,1)S(1)} %bitcast.173), kind=kOutput, calls=%fused_computation.15 | convolution fusion | flops 824174592 | bytes 52740096 | tf_op jit(solution)/shard_map/qhd,khd->hqk/dot_general | solution.py:272
  508.9 22.7 %multiply_convert_fusion.1 = bf16[12,512,1024]{2,1,0:T(8,128)(2,1)} fusion(f32[12,512,1024]{2,1,0:T(8,128)} %get-tuple-element.89, f32[12,512,1024]{2,1,0:T(8,128)} %get-tuple-element.78, f32[12,512]{1,0:T(8,128)S(1)} %get-tuple-element.88, f32[12,512]{1,0:T(8,128)S(1)} %log_add_fusion.1), kind=kLoop, calls=%fused_computation.17 | loop fusion | flops 25165824 | bytes 62963712 | tf_op jit(solution)/shard_map/convert_element_type | solution.py:276
  536.3 15.1 %multiply_convert_fusion = bf16[12,512,1024]{2,1,0:T(8,128)(2,1)} fusion(f32[12,512,1024]{2,1,0:T(8,128)} %get-tuple-element.87, f32[12,512,1024]{2,1,0:T(8,128)S(1)} %bitcast.157, f32[12,512]{1,0:T(8,128)S(1)} %get-tuple-element.86, f32[12,512]{1,0:T(8,128)S(1)} %log_add_fusion), kind=kLoop, calls=%fused_computation.14 | loop fusion | flops 25165824 | bytes 62963712 | tf_op jit(solution)/shard_map/convert_element_type | solution.py:276
  551.4 10.0 %fusion.95 = bf16[512,12,64]{0,2,1:T(8,128)(2,1)} fusion(bf16[1024,12,64]{0,2,1:T(8,128)(2,1)} %bitcast.160, bf16[12,512,1024]{2,1,0:T(8,128)(2,1)} %multiply_convert_fusion.1), kind=kOutput, calls=%fused_computation.139 | convolution fusion | flops 806092800 | bytes 14942208 | tf_op jit(solution)/shard_map/hqk,khd->qhd/dot_general | solution.py:281
  561.4 6.2 fusion.96
  570.4 2.5 convolution_convert_fusion.9
  574.6 6.9 fusion.126
  581.5 6.9 multiply_convert_fusion.3
  589.7 2.5 convolution_convert_fusion.8
  592.2 12.3 %fusion.38 = bf16[1,3072,768]{2,1,0:T(8,128)(2,1)} fusion(bf16[1024,768]{1,0:T(8,128)(2,1)} %bitcast.26, f32[1024,3072]{1,0:T(8,128)} %copy-done.42), kind=kOutput, calls=%fused_computation.62 | convolution fusion | flops 4862509056 | bytes 18874368 | tf_op jit(solution)/shard_map/dot_general | solution.py:53
  606.2 9.1 fusion.37
  615.3 23.0 %copy.72 = bf16[12,512,1024]{1,0,2:T(8,128)(2,1)} copy(bf16[12,512,1024]{2,1,0:T(8,128)(2,1)} %multiply_convert_fusion.1) | data formatting | bytes 25165824 | tf_op jit(solution)/shard_map/convert_element_type | solution.py:276
  638.2 23.1 %copy.73 = bf16[12,512,1024]{1,0,2:T(8,128)(2,1)} copy(bf16[12,512,1024]{2,1,0:T(8,128)(2,1)} %multiply_convert_fusion) | data formatting | bytes 25165824 | tf_op jit(solution)/shard_map/convert_element_type | solution.py:276
  662.9 42.3 %reduce-scatter.10.cloned.1.call-done = bf16[96,768]{1,0:T(8,128)(2,1)} async-done(((bf16[768,768]{1,0:T(8,128)(2,1)}), bf16[96,768]{1,0:T(8,128)(2,1)}) %reduce-scatter.10.cloned.1.call-update) | async-done | bytes 147472 | tf_op jit(solution)/shard_map/reduce_scatter | solution.py:316
  706.6 2.8 fusion.127
  716.0 13.0 %fusion.99 = f32[32,12]{1,0:T(8,128)S(1)} fusion(bf16[12,512,1024]{1,0,2:T(8,128)(2,1)} %copy.72, s32[512,1024]{0,1:T(8,128)} %fusion.57), kind=kOutput, calls=%fused_computation.144 | convolution fusion | flops 419430400 | bytes 14681600 | tf_op jit(solution)/shard_map/hqk,qkc->ch/dot_general | solution.py:294
  729.0 12.4 %fusion.102 = bf16[32,12]{1,0:T(8,128)(2,1)S(1)} fusion(f32[32,12]{1,0:T(8,128)S(1)} %fusion.99, bf16[12,512,1024]{1,0,2:T(8,128)(2,1)} %copy.73, s32[512,1024]{0,1:T(8,128)S(1)} %copy-done.10), kind=kOutput, calls=%fused_computation.147 | convolution fusion | flops 419431168 | bytes 14682368 | tf_op jit(solution)/shard_map/hqk,qkc->ch/dot_general | solution.py:294
  741.4 35.2 %all-reduce.5 = (bf16[768]{0:T(1024)(128)(2,1)S(1)}, bf16[768]{0:T(1024)(128)(2,1)S(1)}, bf16[32,12]{1,0:T(8,128)(2,1)S(1)}) all-reduce(bf16[768]{0:T(1024)(128)(2,1)S(1)} %get-tuple-element.50, bf16[768]{0:T(1024)(128)(2,1)S(1)} %copy-done.37, bf16[32,12]{1,0:T(8,128)(2,1)S(1)} %fusion.102), channel_id=6, replica_groups=mesh['shard'=8,'rep'=4] {'shard'}, use_global_device_ids=true, to_apply=%region_26.27.clone | all-reduce | flops 1920 | bytes 7680
  777.5 6.2 all-reduce.7
  785.9 167.0 %all-reduce.11.cloned.1.call-done = (bf16[96,768]{1,0:T(8,128)(2,1)}, bf16[96,768]{1,0:T(8,128)(2,1)}, bf16[96,768]{1,0:T(8,128)(2,1)}, bf16[96,768]{1,0:T(8,128...) async-done(((bf16[96,768]{1,0:T(8,128)(2,1)}, bf16[96,768]{1,0:T(8,128)(2,1)}, bf16[96,768]{1,0:T(8,128)(2,1)}, bf16[96,768]{1,0:T(8,128)(2,1)}, ...) | async-done | bytes 10027024 | tf_op jit(solution)/shard_map/psum | solution.py:339
  959.7 7.4 broadcast_in_dim.60
  967.1 4.5 broadcast_in_dim.62
  (190 shorter events, 57.7 us)
Async XLA Ops:
  7.2 52.9 %copy-start.26 = (bf16[1024,768]{1,0:T(8,128)(2,1)S(1)}, bf16[1024,768]{1,0:T(8,128)(2,1)}, u32[]{:S(2)}) copy-start(bf16[1024,768]{1,0:T(8,128)(2,1)} %param.14) | copy-start | bytes 4718596
  7.2 150.9 %all-gather.9.cloned.1.call-start = ((), (), s32[]{:S(2)}) async-start(), calls=%async_computation.10 | async-start | bytes 1327104 | tf_op jit(solution)/shard_map/all_gather | solution.py:100
  7.9 154.3 %all-gather.11.cloned.1.call-start = ((), (), s32[]{:S(2)}) async-start(), calls=%async_computation.11 | async-start | bytes 1327104 | tf_op jit(solution)/shard_map/all_gather | solution.py:101
  8.7 183.5 %all-gather.7.cloned.1.call-start = ((), (), s32[]{:S(2)}) async-start(), calls=%async_computation.9 | async-start | bytes 1327104 | tf_op jit(solution)/shard_map/all_gather | solution.py:102
  9.4 235.7 %all-gather.13.cloned.1.call-start = ((), (), s32[]{:S(2)}) async-start(), calls=%async_computation.12 | async-start | bytes 1327104 | tf_op jit(solution)/shard_map/all_gather | solution.py:103
  39.4 152.9 %copy-start.33 = (f32[768]{0:T(1024)}, f32[768]{0:T(1024)S(1)}, u32[]{:S(2)}) copy-start(f32[768]{0:T(1024)S(1)} %convert_element_type.342) | copy-start | bytes 9220
  60.8 131.4 %copy-start.2 = (bf16[1024,768]{0,1:T(8,128)(2,1)}, bf16[1024,768]{0,1:T(8,128)(2,1)S(1)}, u32[]{:S(2)}) copy-start(bf16[1024,768]{0,1:T(8,128)(2,1)S(1)} %copy.60) | copy-start | bytes 4718596
  60.8 3.8 copy-start.9
  61.2 131.1 %copy-start.35 = (f32[1024]{0:T(1024)}, f32[1024]{0:T(1024)S(1)}, u32[]{:S(2)}) copy-start(f32[1024]{0:T(1024)S(1)} %add_rsqrt_fusion.1) | copy-start | bytes 12292
  127.5 30.5 %copy-start.31 = (s32[1024,1]{0,1:T(1,128)S(1)}, s32[1024,1]{0,1:T(1,128)}, u32[]{:S(2)}) copy-start(s32[1024,1]{0,1:T(1,128)} %param.16) | copy-start | bytes 12292
  165.0 41.1 %copy-start.1 = (bf16[1024,768]{0,1:T(8,128)(2,1)}, bf16[1024,768]{0,1:T(8,128)(2,1)S(1)}, u32[]{:S(2)}) copy-start(bf16[1024,768]{0,1:T(8,128)(2,1)S(1)} %convolution_convert_fusion.3) | copy-start | bytes 4718596
  195.0 11.0 %copy-start.16 = (bf16[1024,768]{0,1:T(8,128)(2,1)}, bf16[1024,768]{0,1:T(8,128)(2,1)S(1)}, u32[]{:S(2)}) copy-start(bf16[1024,768]{0,1:T(8,128)(2,1)S(1)} %convolution_convert_fusion.5) | copy-start | bytes 4718596
  195.1 11.0 %copy-start.11 = (bf16[512,768]{0,1:T(8,128)(2,1)S(1)}, bf16[512,768]{0,1:T(8,128)(2,1)}, u32[]{:S(2)}) copy-start(bf16[512,768]{0,1:T(8,128)(2,1)} %get-tuple-element.72) | copy-start | bytes 2359300
  222.2 11.0 %copy-start.17 = (bf16[1024,768]{0,1:T(8,128)(2,1)S(1)}, bf16[1024,768]{0,1:T(8,128)(2,1)}, u32[]{:S(2)}) copy-start(bf16[1024,768]{0,1:T(8,128)(2,1)} %copy-done.16) | copy-start | bytes 4718596
  245.1 3.8 copy-start.32
  249.2 3.1 copy-start.5
  252.4 4.5 copy-start.38
  252.4 62.4 %all-to-all-start = ((bf16[8,128,768]{2,1,0:T(8,128)(2,1)}), bf16[8,128,768]{2,1,0:T(8,128)(2,1)}, u32[]{:S(2)}, u32[]{:S(2)}) async-start(bf16[8,128,768]{2,1,0:T(8,128)(2,1)} %bitcast.185), calls=%async_computation | async-start | bytes 3145728 | tf_op jit(solution)/shard_map/all_to_all | solution.py:193
  314.8 35.1 %all-to-all-start.2 = ((bf16[8,128,768]{2,1,0:T(8,128)(2,1)}), bf16[8,128,768]{2,1,0:T(8,128)(2,1)}, u32[]{:S(2)}, u32[]{:S(2)}) async-start(bf16[8,128,768]{2,1,0:T(8,128)(2,1)} %bitcast.186), calls=%async_computation.2 | async-start | bytes 3145728 | tf_op jit(solution)/shard_map/all_to_all | solution.py:219
  326.6 4.6 copy-start.42
  349.9 38.6 %all-to-all-start.1 = ((bf16[8,128,768]{2,1,0:T(8,128)(2,1)}), bf16[8,128,768]{2,1,0:T(8,128)(2,1)}, u32[]{:S(2)}, u32[]{:S(2)}) async-start(bf16[8,128,768]{2,1,0:T(8,128)(2,1)} %bitcast.187), calls=%async_computation.1 | async-start | bytes 3145728 | tf_op jit(solution)/shard_map/all_to_all | solution.py:198
  369.6 2.7 copy-start.41
  388.5 40.7 %all-to-all-start.3 = ((bf16[8,128,768]{2,1,0:T(8,128)(2,1)}), bf16[8,128,768]{2,1,0:T(8,128)(2,1)}, u32[]{:S(2)}, u32[]{:S(2)}) async-start(bf16[8,128,768]{2,1,0:T(8,128)(2,1)} %bitcast.184), calls=%async_computation.3 | async-start | bytes 3145728 | tf_op jit(solution)/shard_map/all_to_all | solution.py:235
  392.8 270.1 %reduce-scatter.14.cloned.1.call-start = ((), (), s32[]{:S(2)}) async-start(), calls=%async_computation.16 | async-start | bytes 1327104 | tf_op jit(solution)/shard_map/reduce_scatter | solution.py:322
  432.5 1.8 copy-start.22
  432.6 2.4 copy-start.25
  434.9 4.5 copy-start.27
  437.7 1.8 copy-start.7
  439.5 2.9 copy-start.40
  441.9 220.9 %reduce-scatter.12.cloned.1.call-start = ((), (), s32[]{:S(2)}) async-start(), calls=%async_computation.15 | async-start | bytes 1327104 | tf_op jit(solution)/shard_map/reduce_scatter | solution.py:319
  446.7 10.7 %copy-start.14 = (bf16[512,768]{0,1:T(8,128)(2,1)}, bf16[512,768]{0,1:T(8,128)(2,1)S(1)}, u32[]{:S(2)}) copy-start(bf16[512,768]{0,1:T(8,128)(2,1)S(1)} %get-tuple-element.70) | copy-start | bytes 2359300
  474.1 12.2 %copy-start.3 = (bf16[1024,768]{0,1:T(8,128)(2,1)S(1)}, bf16[1024,768]{0,1:T(8,128)(2,1)}, u32[]{:S(2)}) copy-start(bf16[1024,768]{0,1:T(8,128)(2,1)} %copy-done.2) | copy-start | bytes 4718596
  474.1 12.2 %copy-start.34 = (f32[768]{0:T(1024)S(1)}, f32[768]{0:T(1024)}, u32[]{:S(2)}) copy-start(f32[768]{0:T(1024)} %copy-done.33) | copy-start | bytes 9220
  474.1 12.2 %copy-start.36 = (f32[1024]{0:T(1024)S(1)}, f32[1024]{0:T(1024)}, u32[]{:S(2)}) copy-start(f32[1024]{0:T(1024)} %copy-done.35) | copy-start | bytes 12292
  486.3 2.5 copy-start.15
  486.3 2.5 copy-start.18
  508.6 154.3 %reduce-scatter.8.cloned.1.call-start = ((), (), s32[]{:S(2)}) async-start(), calls=%async_computation.13 | async-start | bytes 1327104 | tf_op jit(solution)/shard_map/reduce_scatter | solution.py:313
  508.8 22.8 %slice-start = ((s8[25165824]{0:T(1024)(128)(4,1)}), s8[4194304]{0:T(1024)(128)(4,1)S(1)}, s32[]{:S(2)}) async-start(s8[25165824]{0:T(1024)(128)(4,1)} %bitcast.156), calls=%async_computation.19 | async-start | bytes 8388608
  508.8 22.8 %slice-start.1 = ((s8[25165824]{0:T(1024)(128)(4,1)}), s8[4194304]{0:T(1024)(128)(4,1)S(1)}, s32[]{:S(2)}) async-start(s8[25165824]{0:T(1024)(128)(4,1)} %bitcast.156), calls=%async_computation.20 | async-start | bytes 8388608
  508.8 23.8 %slice-start.2 = ((s8[25165824]{0:T(1024)(128)(4,1)}), s8[4194304]{0:T(1024)(128)(4,1)S(1)}, s32[]{:S(2)}) async-start(s8[25165824]{0:T(1024)(128)(4,1)} %bitcast.156), calls=%async_computation.21 | async-start | bytes 8388608
  508.8 25.0 %slice-start.3 = ((s8[25165824]{0:T(1024)(128)(4,1)}), s8[4194304]{0:T(1024)(128)(4,1)S(1)}, s32[]{:S(2)}) async-start(s8[25165824]{0:T(1024)(128)(4,1)} %bitcast.156), calls=%async_computation.22 | async-start | bytes 8388608
  508.8 26.2 %slice-start.4 = ((s8[25165824]{0:T(1024)(128)(4,1)}), s8[4194304]{0:T(1024)(128)(4,1)S(1)}, s32[]{:S(2)}) async-start(s8[25165824]{0:T(1024)(128)(4,1)} %bitcast.156), calls=%async_computation.23 | async-start | bytes 8388608
  508.8 27.5 %slice-start.5 = ((s8[25165824]{0:T(1024)(128)(4,1)}), s8[4194304]{0:T(1024)(128)(4,1)S(1)}, s32[]{:S(2)}) async-start(s8[25165824]{0:T(1024)(128)(4,1)} %bitcast.156), calls=%async_computation.24 | async-start | bytes 8388608
  551.4 10.0 %copy-start = (bf16[12,512,1024]{2,1,0:T(8,128)(2,1)S(1)}, bf16[12,512,1024]{2,1,0:T(8,128)(2,1)}, u32[]{:S(2)}) copy-start(bf16[12,512,1024]{2,1,0:T(8,128)(2,1)} %multiply_convert_fusion) | copy-start | bytes 37748740
  567.6 2.8 copy-start.4
  569.3 1.1 copy-start.28
  570.4 4.1 copy-start.13
  573.0 132.2 %reduce-scatter.10.cloned.1.call-start = ((), (), s32[]{:S(2)}) async-start(), calls=%async_computation.14 | async-start | bytes 1327104 | tf_op jit(solution)/shard_map/reduce_scatter | solution.py:316
  574.5 7.0 copy-start.12
  588.5 1.2 copy-start.23
  592.2 12.4 %copy-start.6 = (bf16[1024,768]{0,1:T(8,128)(2,1)S(1)}, bf16[1024,768]{0,1:T(8,128)(2,1)}, u32[]{:S(2)}) copy-start(bf16[1024,768]{0,1:T(8,128)(2,1)} %copy-done.5) | copy-start | bytes 4718596
  592.2 184.6 %reduce-scatter.16.cloned.1.call-start = ((), (), s32[]{:S(2)}) async-start(), calls=%async_computation.17 | async-start | bytes 221184
  605.9 347.1 %all-reduce.11.cloned.1.call-start = ((), (), s32[]{:S(2)}) async-start(), calls=%async_computation.18 | async-start | bytes 20054016 | tf_op jit(solution)/shard_map/psum | solution.py:339
  638.2 23.1 %copy-start.21 = (bf16[1024,768]{0,1:T(8,128)(2,1)S(1)}, bf16[1024,768]{0,1:T(8,128)(2,1)}, u32[]{:S(2)}) copy-start(bf16[1024,768]{0,1:T(8,128)(2,1)} %get-tuple-element.68) | copy-start | bytes 4718596
  705.2 1.4 copy-start.29
  706.6 2.8 copy-start.24
  706.6 2.8 copy-start.39
  709.4 1.4 copy-start.20
  709.5 1.7 copy-start.30
  711.2 2.2 copy-start.8
  716.0 13.0 %copy-start.10 = (s32[512,1024]{0,1:T(8,128)S(1)}, s32[512,1024]{0,1:T(8,128)}, u32[]{:S(2)}) copy-start(s32[512,1024]{0,1:T(8,128)} %fusion.58) | copy-start | bytes 6291460
  729.0 12.4 %copy-start.37 = (bf16[768]{0:T(1024)(128)(2,1)S(1)}, bf16[768]{0:T(1024)(128)(2,1)}, u32[]{:S(2)}) copy-start(bf16[768]{0:T(1024)(128)(2,1)} %get-tuple-element.48) | copy-start | bytes 4612
  957.9 9.2 slice-start.6
  959.7 7.4 slice-start.7
  (1 other events, 1.1 us)
Sparse Core Ops, SparseCore 0:
  10.2 43.8 all-gather.8
  56.3 39.8 all-gather.10
  98.3 39.8 all-gather.6
  140.2 39.8 all-gather.12
  442.1 63.3 reduce-scatter.13
  508.7 63.3 reduce-scatter.11
  575.6 63.0 reduce-scatter.7
  642.1 63.1 reduce-scatter.9
  709.0 60.0 reduce-scatter.15
  772.7 180.2 all-reduce.10
where the time goes:
time: 992 us; the launch traced here: 979 us
  matrix products  316 us (32%)
  waiting for transfers between devices  258 us (26%)
  local copies, waits for them, and re-layouts  141 us (14%)
  blocking collectives  130 us (13%)
  other arithmetic  97.3 us (10%)
  starting transfers between devices  19.2 us (2%)
  between operations  18 us (2%)
    psum x1, waiting for transfers between devices, on_device(): lax.psum(group_sums[0].astype(jnp.bfloat16), 'rep').astype(jnp.float32)  167 us
    dot_general x14, matrix products, contract(): lax.dot_general(left_side, right_side, (((left_axis,), (right_axis,)), ((...  67 us
    dot_general x2, local copies, waits for them, and re-layouts, block_scores(): jnp.einsum('qkc,ch->hqk', onehot, table_low, preferred_element_type=jnp.f...  60.8 us
    unnamed x2, blocking collectives  58.3 us
    all_gather x1, blocking collectives, on_device(): lax.all_gather(router_weight, 'shard', axis=0, tiled=True)  48.8 us
    convert_element_type x2, local copies, waits for them, and re-layouts, on_device(): score_grad = (probs_block * (prob_grad - row_delta)).astype(jnp.bfloat16)  46 us
    reduce_scatter x1, waiting for transfers between devices, on_device(): lax.psum_scatter(key_grad.astype(jnp.bfloat16), 'shard', scatter_dimensio...  42.3 us
    convert_element_type x2, other arithmetic, on_device(): score_grad = (probs_block * (prob_grad - row_delta)).astype(jnp.bfloat16)  37.8 us
  transfers between devices with their start and end apart: 14, of which 5 were waited for; matrix products, arithmetic and copies ran while one was open for 51% of the time, Pallas kernels for 0%

commit v1 on v0

v1 whole, which is shorter than its diff:
```python
import jax
import jax.numpy as jnp
import numpy as np
from jax import lax
from jax.experimental import pallas as pl
from jax.experimental.pallas import tpu as pltpu
from jax.sharding import PartitionSpec as P

MAX_DISTANCE = 128
EPSILON = 1e-06
MASKED = -1000000000.0
TILE = 128
QUERY_BLOCK = 256


def contract(left_side, right_side, left_axis, right_axis):
    return lax.dot_general(
        left_side,
        right_side,
        (((left_axis,), (right_axis,)), ((), ())),
        preferred_element_type=jnp.float32,
    )


def offset_buckets(bucket_count, reach):
    half_count = bucket_count // 2
    exact_count = half_count // 2
    offset_list = -(np.arange(4 * TILE) - 2 * TILE)
    distance = np.abs(offset_list)
    spread_log = (
        np.log(np.maximum(distance, 1) / exact_count)
        / np.log(reach / exact_count)
        * (half_count - exact_count)
    )
    far_bucket = np.minimum(
        exact_count + np.maximum(spread_log, 0.0).astype(np.int64), half_count - 1
    )
    return (offset_list > 0) * half_count + np.where(
        distance < exact_count, distance, far_bucket
    )


def fill_strip(strip_ref, offsets, slot_count):
    base = slot_count - TILE
    wide = pltpu.roll(
        jnp.broadcast_to(offsets, (TILE, 4 * TILE)), 0, 1, stride=1, stride_axis=0
    )
    strip_ref[: base - TILE, :] = jnp.broadcast_to(
        offsets[:, 4 * TILE - 1 : 4 * TILE], (base - TILE, TILE)
    )
    for shift in (-1, 0, 1):
        first = (2 - shift) * TILE
        row = base + shift * TILE
        strip_ref[row : row + TILE, :] = wide[:, first : first + TILE]
    strip_ref[base + 2 * TILE :, :] = jnp.broadcast_to(
        offsets[:, 0:1], (slot_count - 2 * TILE, TILE)
    )


def biased(strip_ref, scores, first_row, slot_count):
    parts = []
    for part in range(QUERY_BLOCK // TILE):
        start = slot_count - TILE - first_row - part * TILE
        parts.append(
            scores[:, part * TILE : (part + 1) * TILE]
            + strip_ref[start : start + slot_count, :]
        )
    return jnp.concatenate(parts, axis=1)


def attend_kernel(q_ref, k_ref, v_ref, mask_ref, offset_ref, out_ref, log_ref, strip_ref):
    slot_count, width = q_ref.shape
    head_size = width // 2
    lane = lax.broadcasted_iota(jnp.int32, (QUERY_BLOCK, width), 1)
    one_lane = (lane == 0).astype(jnp.bfloat16)
    keys = jnp.concatenate([k_ref[...], mask_ref[...]], axis=1)
    values_turned = jnp.concatenate(
        [v_ref[...].T, jnp.ones((16, slot_count), jnp.bfloat16)], axis=0
    )
    for half in range(2):
        fill_strip(strip_ref.at[half], offset_ref[0, half : half + 1, :], slot_count)
    for first_row in range(0, slot_count, QUERY_BLOCK):
        rows = slice(first_row, first_row + QUERY_BLOCK)
        q_block = q_ref[rows, :] * jnp.bfloat16(0.125)
        pieces = []
        for half in range(2):
            mine = (lane // head_size) == half
            q_half = jnp.concatenate(
                [jnp.where(mine, q_block, jnp.bfloat16(0)), one_lane], axis=1
            )
            scores = biased(strip_ref.at[half], contract(keys, q_half, 1, 1), first_row, slot_count)
            peak = jnp.max(scores, axis=0, keepdims=True)
            weights = jnp.exp(scores - peak).astype(jnp.bfloat16)
            mixed = jnp.dot(values_turned, weights, preferred_element_type=jnp.float32)
            total = mixed[width : width + 1, :]
            pieces.append(mixed[half * head_size : (half + 1) * head_size, :] / total)
            log_ref[0, half : half + 1, rows] = peak + jnp.log(total)
        out_ref[rows, :] = jnp.concatenate(pieces, axis=0).T.astype(jnp.bfloat16)


def attend_back_kernel(
    q_ref, k_ref, v_ref, mask_ref, offset_ref, log_ref, out_ref, grad_ref,
    dq_ref, dk_ref, dv_ref, table_ref, strip_ref, sum_ref,
):
    slot_count, width = q_ref.shape
    head_size = width // 2
    lane = lax.broadcasted_iota(jnp.int32, (QUERY_BLOCK, width), 1)
    one_lane = (lane == 0).astype(jnp.bfloat16)
    keys = jnp.concatenate([k_ref[...], mask_ref[...]], axis=1)
    keys_turned = k_ref[...].T
    values = v_ref[...]
    for half in range(2):
        fill_strip(strip_ref.at[half], offset_ref[0, half : half + 1, :], slot_count)
    sum_ref[...] = jnp.zeros(sum_ref.shape, jnp.float32)
    key_total = jnp.zeros((slot_count, width), jnp.float32)
    value_total = jnp.zeros((slot_count, width), jnp.float32)
    for first_row in range(0, slot_count, QUERY_BLOCK):
        rows = slice(first_row, first_row + QUERY_BLOCK)
        q_block = q_ref[rows, :] * jnp.bfloat16(0.125)
        grad_block = grad_ref[rows, :]
        product = (
            grad_block.astype(jnp.float32) * out_ref[rows, :].astype(jnp.float32)
        ).T
        pieces = []
        weights_parts, score_parts, q_parts, grad_parts = [], [], [], []
        for half in range(2):
            mine = (lane // head_size) == half
            q_own = jnp.where(mine, q_block, jnp.bfloat16(0))
            grad_own = jnp.where(mine, grad_block, jnp.bfloat16(0))
            delta = jnp.sum(
                product[half * head_size : (half + 1) * head_size, :], axis=0, keepdims=True
            )
            q_half = jnp.concatenate([q_own, one_lane], axis=1)
            scores = biased(strip_ref.at[half], contract(keys, q_half, 1, 1), first_row, slot_count)
            weights = jnp.exp(scores - log_ref[0, half : half + 1, rows])
            prob_grad = contract(values, grad_own, 1, 1)
            score_grad = weights * (prob_grad - delta)
            for part in range(QUERY_BLOCK // TILE):
                start = slot_count - TILE - first_row - part * TILE
                sum_ref[half, start : start + slot_count, :] += score_grad[
                    :, part * TILE : (part + 1) * TILE
                ]
            score_low = score_grad.astype(jnp.bfloat16)
            turned = jnp.dot(keys_turned, score_low, preferred_element_type=jnp.float32)
            pieces.append(turned[half * head_size : (half + 1) * head_size, :] * 0.125)
            weights_parts.append(weights.astype(jnp.bfloat16))
            score_parts.append(score_low)
            q_parts.append(q_own)
            grad_parts.append(grad_own)
        dq_ref[rows, :] = jnp.concatenate(pieces, axis=0).T.astype(jnp.bfloat16)
        key_total = key_total + jnp.dot(
            jnp.concatenate(score_parts, axis=1),
            jnp.concatenate(q_parts, axis=0),
            preferred_element_type=jnp.float32,
        )
        value_total = value_total + jnp.dot(
            jnp.concatenate(weights_parts, axis=1),
            jnp.concatenate(grad_parts, axis=0),
            preferred_element_type=jnp.float32,
        )
    dk_ref[...] = key_total.astype(jnp.bfloat16)
    dv_ref[...] = value_total.astype(jnp.bfloat16)
    base = slot_count - TILE
    table_ref[...] = jnp.zeros(table_ref.shape, jnp.float32)
    for half in range(2):
        sums = sum_ref.at[half]
        wide = jnp.concatenate(
            [jnp.zeros((TILE, TILE), jnp.float32)]
            + [sums[base + shift * TILE : base + (shift + 1) * TILE, :] for shift in (1, 0, -1)],
            axis=1,
        )
        level = wide
        row = lax.broadcasted_iota(jnp.int32, wide.shape, 0)
        amount = 1
        while amount < TILE:
            level = jnp.where(
                (row // amount) % 2 == 1, pltpu.roll(level, 4 * TILE - amount, 1), level
            )
            amount *= 2
        table_ref[0, half : half + 1, :] = jnp.sum(level, axis=0, keepdims=True)
        far_left = jnp.sum(sums[: base - TILE, :], axis=0, keepdims=True)
        far_right = jnp.sum(sums[base + 2 * TILE :, :], axis=0, keepdims=True)
        table_ref[0, 2 + half : 3 + half, :] = jnp.concatenate(
            [far_left, far_right, jnp.zeros((1, 2 * TILE), jnp.float32)], axis=1
        )


def pair_specs(slot_count):
    column = pl.BlockSpec((slot_count, 2 * 64), lambda p: (0, p))
    mask = pl.BlockSpec((slot_count, TILE), lambda p: (0, 0))
    small = lambda rows, lanes: pl.BlockSpec((1, rows, lanes), lambda p: (p, 0, 0))
    return column, mask, small


def attend(queries, keys, values, mask, offsets):
    slot_count, model_width = queries.shape
    pairs = offsets.shape[0]
    column, mask_spec, small = pair_specs(slot_count)
    strip = pltpu.VMEM((2, 2 * slot_count - TILE, TILE), jnp.float32)
    return pl.pallas_call(
        attend_kernel,
        grid=(pairs,),
        in_specs=[column, column, column, mask_spec, small(2, 4 * TILE)],
        out_specs=[column, small(2, slot_count)],
        out_shape=[
            jax.ShapeDtypeStruct((slot_count, model_width), jnp.bfloat16),
            jax.ShapeDtypeStruct((pairs, 2, slot_count), jnp.float32),
        ],
        scratch_shapes=[strip],
        compiler_params=pltpu.CompilerParams(vmem_limit_bytes=50 * 2**20),
        cost_estimate=pl.CostEstimate(
            flops=2 * pairs * slot_count * slot_count * 800,
            bytes_accessed=8 * slot_count * model_width,
            transcendentals=2 * pairs * slot_count * slot_count,
        ),
        name="attend",
    )(queries, keys, values, mask, offsets)


def attend_back(queries, keys, values, mask, offsets, logs, attended, grad):
    slot_count, model_width = queries.shape
    pairs = offsets.shape[0]
    column, mask_spec, small = pair_specs(slot_count)
    strip = pltpu.VMEM((2, 2 * slot_count - TILE, TILE), jnp.float32)
    wide = jax.ShapeDtypeStruct((slot_count, model_width), jnp.bfloat16)
    return pl.pallas_call(
        attend_back_kernel,
        grid=(pairs,),
        in_specs=[
            column, column, column, mask_spec, small(2, 4 * TILE), small(2, slot_count),
            column, column,
        ],
        out_specs=[column, column, column, small(4, 4 * TILE)],
        out_shape=[
            wide, wide, wide, jax.ShapeDtypeStruct((pairs, 4, 4 * TILE), jnp.float32)
        ],
        scratch_shapes=[strip, strip],
        compiler_params=pltpu.CompilerParams(vmem_limit_bytes=56 * 2**20),
        cost_estimate=pl.CostEstimate(
            flops=2 * pairs * slot_count * slot_count * 1600,
            bytes_accessed=16 * slot_count * model_width,
            transcendentals=2 * pairs * slot_count * slot_count,
        ),
        name="attend_back",
    )(queries, keys, values, mask, offsets, logs, attended, grad)


def spread_table(table):
    bucket_count, head_count = table.shape
    hot = (
        offset_buckets(bucket_count, MAX_DISTANCE)[None, :] == np.arange(bucket_count)[:, None]
    )
    spread = contract(table, jnp.asarray(hot, jnp.bfloat16), 0, 0)
    return spread.reshape(head_count // 2, 2, 4 * TILE)


def collect_table(sums, bucket_count):
    pairs = sums.shape[0]
    buckets = offset_buckets(bucket_count, MAX_DISTANCE)
    near = sums[:, :2, :].reshape(2 * pairs, 4 * TILE)
    far = sums[:, 2:, : 2 * TILE].reshape(2 * pairs, 2 * TILE)
    hot = buckets[:, None] == np.arange(bucket_count)[None, :]
    far_buckets = np.where(np.arange(2 * TILE) < TILE, buckets[-1], buckets[0])
    far_hot = far_buckets[:, None] == np.arange(bucket_count)[None, :]
    both = jnp.concatenate([near, far], axis=1)
    both_hot = jnp.asarray(np.concatenate([hot, far_hot], axis=0), jnp.float32)
    return lax.dot_general(
        both_hot, both, (((0,), (1,)), ((), ())), precision=lax.Precision.HIGHEST,
        preferred_element_type=jnp.float32,
    )


def rms_forward(values, gain):
    inverse = lax.rsqrt(jnp.mean(values * values, axis=-1, keepdims=True) + EPSILON)
    return (values * inverse * gain, inverse)


def rms_backward(values, inverse, gain, upstream):
    scaled = upstream * gain
    gain_grad = jnp.sum(upstream * values * inverse, axis=0)
    inner_mean = jnp.mean(scaled * values, axis=-1, keepdims=True)
    return (inverse * scaled - values * inverse * inverse * inverse * inner_mean, gain_grad)


def pack_small(parts, width):
    flat = jnp.concatenate([part.reshape(-1) for part in parts])
    rows = -(-flat.shape[0] // width)
    return jnp.pad(flat, (0, rows * width - flat.shape[0])).reshape(rows, width)


def gather_packed(packed, group_size):
    replicas = lax.axis_size("rep")
    rows, width = packed.shape
    part = -(-rows // replicas)
    packed = jnp.pad(packed, ((0, part * replicas - rows), (0, 0)))
    own = lax.dynamic_slice_in_dim(packed, lax.axis_index("rep") * part, part, 0)
    whole = lax.all_gather(own, ("shard", "rep"), axis=0)
    return whole.reshape(group_size, part * replicas, width)[:, :rows]


def replica_sum(value):
    return lax.psum(value, "rep")


def on_device(
    tokens,
    lengths,
    expert_choice,
    query_weight,
    key_weight,
    value_weight,
    output_weight,
    first_gain,
    second_gain,
    router_weight,
    bias_table,
    expert_in,
    expert_out,
    cotangent,
):
    token_count, model_width = tokens.shape
    group_size = lax.axis_size("shard")
    expert_count = router_weight.shape[1]
    capacity = token_count // group_size
    bucket_count = bias_table.shape[0] * group_size
    shard_rows = query_weight.shape[0]
    live_mask = jnp.arange(token_count, dtype=jnp.int32) < lengths[0]
    small_parts = (router_weight, first_gain, second_gain, bias_table)
    packed = jnp.concatenate(
        [
            query_weight,
            key_weight,
            value_weight,
            output_weight,
            pack_small(small_parts, model_width),
        ],
        axis=0,
    )
    whole = gather_packed(packed, group_size)
    full_query, full_key, full_value, full_output = (
        whole[:, index * shard_rows : (index + 1) * shard_rows].reshape(-1, model_width)
        for index in range(4)
    )
    small = whole[:, 4 * shard_rows :].reshape(group_size, -1)
    unpacked = []
    position = 0
    for part in small_parts:
        unpacked.append(
            small[:, position : position + part.size].reshape((-1,) + part.shape[1:])
        )
        position += part.size
    full_router, first_low, second_low_gain, table_low = unpacked
    first_scale = first_low.astype(jnp.float32)
    second_scale = second_low_gain.astype(jnp.float32)
    inputs = tokens.astype(jnp.float32)
    normed, first_inverse = rms_forward(inputs, first_scale)
    normed_low = normed.astype(jnp.bfloat16)
    queries = jnp.dot(normed_low, full_query, preferred_element_type=jnp.float32).astype(
        jnp.bfloat16
    )
    keys_low = jnp.dot(normed_low, full_key, preferred_element_type=jnp.float32).astype(
        jnp.bfloat16
    )
    values_low = jnp.dot(normed_low, full_value, preferred_element_type=jnp.float32).astype(
        jnp.bfloat16
    )
    key_mask = jnp.broadcast_to(
        jnp.where(live_mask, 0.0, MASKED)[:, None], (token_count, TILE)
    ).astype(jnp.bfloat16)
    offsets = spread_table(table_low)
    attended, logs = attend(queries, keys_low, values_low, key_mask, offsets)
    middle = inputs + jnp.dot(attended, full_output, preferred_element_type=jnp.float32)
    second, second_inverse = rms_forward(middle, second_scale)
    second_low = second.astype(jnp.bfloat16)
    logits = jnp.dot(second_low, full_router, preferred_element_type=jnp.float32)
    router_probs = jax.nn.softmax(logits, axis=-1)
    choice_hot = expert_choice == jnp.arange(expert_count, dtype=jnp.int32)[None, :]
    gates = jnp.sum(jnp.where(choice_hot, router_probs, 0.0), axis=1)
    hot_live = (choice_hot & live_mask[:, None]).astype(jnp.int32)
    before = jnp.cumsum(hot_live, axis=0) - hot_live
    slot = jnp.sum(before * hot_live, axis=1)
    kept = live_mask & (slot < capacity)
    target = jnp.where(kept, expert_choice[:, 0] * capacity + slot, -1)
    dispatch = (
        target[None, :] == jnp.arange(expert_count * capacity, dtype=jnp.int32)[:, None]
    ).astype(jnp.bfloat16)

    def exchange(rows):
        return lax.all_to_all(
            rows.reshape(expert_count, capacity, model_width),
            "shard",
            split_axis=0,
            concat_axis=0,
            tiled=True,
        ).reshape(-1, model_width)

    send_rows = jnp.dot(dispatch, second_low, preferred_element_type=jnp.float32).astype(
        jnp.bfloat16
    )
    upstream = cotangent.astype(jnp.float32) * live_mask[:, None].astype(jnp.float32)
    result_grad = (gates[:, None] * upstream).astype(jnp.bfloat16)
    send_grad = jnp.dot(dispatch, result_grad, preferred_element_type=jnp.float32).astype(
        jnp.bfloat16
    )
    weight_in = expert_in[0]
    weight_out = expert_out[0]
    received = exchange(send_rows)
    arrived = exchange(send_grad)
    inner = jnp.dot(received, weight_in, preferred_element_type=jnp.float32)
    active_value, active_pull = jax.vjp(jax.nn.gelu, inner)
    active = active_value.astype(jnp.bfloat16)
    produced = jnp.dot(active, weight_out, preferred_element_type=jnp.float32).astype(jnp.bfloat16)
    returned = exchange(produced)
    out_weight_grad = contract(active, arrived, 0, 0).astype(jnp.bfloat16)
    out_total = replica_sum(out_weight_grad[None])
    active_grad = contract(arrived, weight_out, 1, 1)
    inner_grad = active_pull(active_grad)[0].astype(jnp.bfloat16)
    in_weight_grad = contract(received, inner_grad, 0, 0).astype(jnp.bfloat16)
    in_total = replica_sum(in_weight_grad[None])
    rows_grad = contract(inner_grad, weight_in, 1, 1).astype(jnp.bfloat16)
    rows_back = exchange(rows_grad)
    combined = contract(dispatch, returned, 0, 0)
    layer_out = (middle + gates[:, None] * combined).astype(jnp.bfloat16)
    gate_grad = jnp.sum(upstream * combined, axis=1)
    chosen_float = choice_hot.astype(jnp.float32)
    logit_grad = (
        router_probs * (chosen_float * gate_grad[:, None] - (gates * gate_grad)[:, None])
    ).astype(jnp.bfloat16)
    router_grad = contract(second_low, logit_grad, 0, 0)
    second_grad = contract(logit_grad, full_router, 1, 1) + contract(dispatch, rows_back, 0, 0)
    middle_part, second_gain_grad = rms_backward(middle, second_inverse, second_scale, second_grad)
    middle_grad = upstream + middle_part
    branch_grad = middle_grad.astype(jnp.bfloat16)
    output_grad = contract(attended, branch_grad, 0, 0)
    attended_grad = contract(branch_grad, full_output, 1, 1).astype(jnp.bfloat16)
    query_low, key_low, value_low, table_sums = attend_back(
        queries, keys_low, values_low, key_mask, offsets, logs, attended, attended_grad
    )
    table_grad = collect_table(table_sums, bucket_count)
    query_grad = contract(normed_low, query_low, 0, 0)
    key_grad = contract(normed_low, key_low, 0, 0)
    value_grad = contract(normed_low, value_low, 0, 0)
    normed_grad = (
        contract(query_low, full_query, 1, 1)
        + contract(key_low, full_key, 1, 1)
        + contract(value_low, full_value, 1, 1)
    )
    input_part, first_gain_grad = rms_backward(inputs, first_inverse, first_scale, normed_grad)
    token_grad = (middle_grad + input_part).astype(jnp.bfloat16)
    small_grads = (router_grad, first_gain_grad, second_gain_grad, table_grad)
    small_rows = jnp.concatenate(
        [grad.astype(jnp.bfloat16).reshape(group_size, -1) for grad in small_grads], axis=1
    )
    small_height = -(-small_rows.shape[1] // model_width)
    small_rows = jnp.pad(
        small_rows, ((0, 0), (0, small_height * model_width - small_rows.shape[1]))
    ).reshape(group_size, small_height, model_width)
    grads = jnp.concatenate(
        [
            grad.astype(jnp.bfloat16).reshape(group_size, shard_rows, model_width)
            for grad in (query_grad, key_grad, value_grad, output_grad)
        ]
        + [small_rows],
        axis=1,
    )
    group_sum = lax.psum_scatter(grads, "shard", scatter_dimension=0, tiled=True)
    group_sum, in_total, out_total = lax.optimization_barrier((group_sum, in_total, out_total))
    total = replica_sum(group_sum)[0].astype(jnp.float32)
    weight_totals = [
        total[index * shard_rows : (index + 1) * shard_rows] for index in range(4)
    ]
    flat = total[4 * shard_rows :].reshape(-1)
    small_totals = []
    position = 0
    for part in small_parts:
        small_totals.append(flat[position : position + part.size].reshape(part.shape))
        position += part.size
    router_total, first_total, second_total, table_total = small_totals
    return (
        layer_out,
        token_grad,
        *weight_totals,
        first_total,
        second_total,
        router_total,
        table_total,
        in_total.astype(jnp.float32),
        out_total.astype(jnp.float32),
    )


def solution(mesh):
    placed = (
        P(("shard", "rep"), None),
        P(("shard", "rep")),
        P(("shard", "rep"), None),
        P("shard", None),
        P("shard", None),
        P("shard", None),
        P("shard", None),
        P("shard"),
        P("shard"),
        P("shard", None),
        P("shard", None),
        P("shard", None, None),
        P("shard", None, None),
        P(("shard", "rep"), None),
    )
    return jax.shard_map(
        on_device,
        mesh=mesh,
        in_specs=placed,
        out_specs=(
            P(("shard", "rep"), None),
            P(("shard", "rep"), None),
            P("shard", None),
            P("shard", None),
            P("shard", None),
            P("shard", None),
            P("shard"),
            P("shard"),
            P("shard", None),
            P("shard", None),
            P("shard", None, None),
            P("shard", None, None),
        ),
        check_vma=False,
    )
```

time: 992 us -> 613 us (0.62)
  matrix products: 316 us -> 109 us
  blocking collectives: 130 us -> 0 us
  local copies, waits for them, and re-layouts: 141 us -> 44.2 us
  other arithmetic: 97.3 us -> 23.8 us
  Pallas kernels: 0 us -> 72.8 us
  waiting for transfers between devices: 258 us -> 320 us
    dot_general x20 -> x4, matrix products: 221 us -> 12 us  [the longest x1 7.36 us: on_device(): inner = jnp.dot(received, weight_in, preferred_element_type=jnp.float32)]
    psum x1 -> x2, waiting for transfers between devices: 167 us -> 87 us  [replica_sum(): return lax.psum(value, 'rep')]
    pallas_call x0 -> x2, Pallas kernels: none -> 72.8 us  [the longest x1 38.8 us: attend_back(): pl.pallas_call(attend_back_kernel, grid=(pairs,), in_specs=[column, colum...]
    all_gather x2 -> x0, blocking collectives: 65.4 us -> none  [the longest x1 48.8 us: on_device(): lax.all_gather(router_weight, 'shard', axis=0, tiled=True)]
    all_gather x4 -> x1, waiting for transfers between devices: 0.05 us -> 62.3 us  [gather_packed(): whole = lax.all_gather(own, ('shard', 'rep'), axis=0)]
    dot_general x2 -> x3, local copies, waits for them, and re-layouts: 60.8 us -> 0.13 us  [contract(): lax.dot_general(left_side, right_side, (((left_axis,), (right_axis,)), ((...]
    reduce_scatter x4 -> x1, waiting for transfers between devices: 42.3 us -> 102 us  [on_device(): lax.psum_scatter(grads, 'shard', scatter_dimension=0, tiled=True)]
    unnamed x2 -> x0, blocking collectives: 58.3 us -> none
  transfers between devices with their start and end apart: 14 -> 8, of which waited for: 5 -> 8; matrix products, arithmetic and copies ran while one was open for 51% -> 22% of each run, Pallas kernels for 0% -> 6%
where the time goes in v1:
time: 613 us; the launch traced here: 603 us
  waiting for transfers between devices  320 us (52%)
  matrix products  109 us (18%)
  Pallas kernels  72.8 us (12%)
  local copies, waits for them, and re-layouts  44.2 us (7%)
  other arithmetic  23.8 us (4%)
  starting transfers between devices  18 us (3%)
  between operations  15.5 us (3%)
    reduce_scatter x1, waiting for transfers between devices, on_device(): lax.psum_scatter(grads, 'shard', scatter_dimension=0, tiled=True)  102 us
    psum x2, waiting for transfers between devices, replica_sum(): return lax.psum(value, 'rep')  87 us
    dot_general x17, matrix products, contract(): lax.dot_general(left_side, right_side, (((left_axis,), (right_axis,)), ((...  72.7 us
    all_to_all x4, waiting for transfers between devices, exchange(): lax.all_to_all(rows.reshape(expert_count, capacity, model_width), 'shard'...  69.3 us
    all_gather x1, waiting for transfers between devices, gather_packed(): whole = lax.all_gather(own, ('shard', 'rep'), axis=0)  62.3 us
    pallas_call x1, Pallas kernels, attend_back(): pl.pallas_call(attend_back_kernel, grid=(pairs,), in_specs=[column, colum...  38.8 us
    pallas_call x1, Pallas kernels, attend(): pl.pallas_call(attend_kernel, grid=(pairs,), in_specs=[column, column, co...  34 us
    unnamed x91, local copies, waits for them, and re-layouts  24.3 us
  transfers between devices with their start and end apart: 8, of which 8 were waited for; matrix products, arithmetic and copies ran while one was open for 22% of the time, Pallas kernels for 6%

profile of v1, /device:TPU:0, one launch (start us, length us, event | category | flops | bytes accessed | tf_op | source)
XLA Modules:
  0.0 603.4 jit_solution(8147528677611756218)
XLA Ops:
  7.2 0.9 reshape.235
  8.1 0.8 copy.58
  9.8 0.9 constant_dynamic-update-slice_fusion.4
  10.7 0.9 constant_dynamic-update-slice_fusion.3
  11.6 0.9 constant_dynamic-update-slice_fusion.2
  12.6 0.9 constant_dynamic-update-slice_fusion.1
  15.6 2.3 reduce-window.6
  19.6 62.3 %all-gather.4.cloned.1.call-done = bf16[32,97,768]{2,1,0:T(8,128)(2,1)} async-done(((bf16[1,97,768]{2,1,0:T(8,128)(2,1)}), bf16[32,97,768]{2,1,0:T(8,128)(2,1)}) %all-gather.4.cloned.1.call-update) | async-done | bytes 4767760 | tf_op jit(solution)/shard_map/all_gather | solution.py:297
  81.9 7.4 %reshape.237 = bf16[8,388,768]{2,1,0:T(8,128)(2,1)} reshape(bf16[32,97,768]{2,1,0:T(8,128)(2,1)} %all-gather.4.cloned.1.call-done) | data formatting | bytes 9535488 | tf_op jit(solution)/shard_map/reshape | solution.py:298
  89.3 0.9 slice_bitcast_fusion.4
  90.2 4.2 fusion.85
  95.1 4.0 convolution_convert_fusion.4.k_ref
  99.0 2.7 convolution_convert_fusion.3.v_ref
  101.8 1.6 convolution_convert_fusion.5.q_ref
  103.6 34.0 %attend.1 = (bf16[1024,768]{1,0:T(8,128)(2,1)S(1)}, f32[6,2,1024]{2,1,0:T(2,128)S(1)}) custom-call(bf16[1024,768]{1,0:T(8,128)(2,1)S(1)} %convolution_convert_fusion.5.q_ref, bf16[1024,768]{1,0:T(8,128)(2,1)} %convolution_convert_fusion.4.k_ref, bf16[1024,768]{1,0:T(8,128)(2,1)} %convolution_convert_fusion.3.v_ref, ...), custom_call_target="tpu_custom_call" | custom-call | flops 10066329600 | bytes 6291456 | tf_op jit(solution)/shard_map/attend/pallas_call | solution.py:200
  137.7 1.7 multiply_reduce_fusion.3
  139.8 3.1 fusion.39
  142.9 4.4 all-to-all-start
  147.2 1.7 copy.62
  149.7 3.2 fusion.40
  152.9 32.0 %all-to-all-done = bf16[8,128,768]{2,1,0:T(8,128)(2,1)} async-done(((bf16[8,128,768]{2,1,0:T(8,128)(2,1)}), bf16[8,128,768]{2,1,0:T(8,128)(2,1)}, u32[]{:S(2)}, u32[]{:S(2)}) %all-to-all-start) | async-done | bytes 1572896 | tf_op jit(solution)/shard_map/all_to_all | solution.py:389
  184.9 4.3 all-to-all-start.2
  189.2 7.4 %fusion.13 = f32[1024,3072]{1,0:T(8,128)S(1)} fusion(bf16[1024,768]{1,0:T(8,128)(2,1)} %bitcast.12, bf16[1,768,3072]{2,1,0:T(8,128)(2,1)} %param.27), kind=kOutput, calls=%fused_computation.23 | convolution fusion | flops 4831838208 | bytes 18874368 | tf_op jit(solution)/shard_map/dot_general | solution.py:409
  196.6 4.5 copy-done.34
  201.1 10.8 %fusion.44 = bf16[1024,768]{1,0:T(8,128)(2,1)} fusion(bf16[1,3072,768]{2,1,0:T(8,128)(2,1)} %param.28, f32[1024,3072]{1,0:T(8,128)S(1)} %fusion.13), kind=kOutput, calls=%fused_computation.62 | convolution fusion | flops 4860936192 | bytes 18874368 | tf_op jit(solution)/shard_map/dot_general | solution.py:412
  211.9 14.0 %all-to-all-done.2 = bf16[8,128,768]{2,1,0:T(8,128)(2,1)} async-done(((bf16[8,128,768]{2,1,0:T(8,128)(2,1)}), bf16[8,128,768]{2,1,0:T(8,128)(2,1)}, u32[]{:S(2)}, u32[]{:S(2)}) %all-to-all-start.2) | async-done | bytes 1572896 | tf_op jit(solution)/shard_map/all_to_all | solution.py:389
  225.9 4.7 all-to-all-start.1
  230.6 15.4 %fusion.6 = bf16[1024,3072]{1,0:T(8,128)(2,1)S(1)} fusion(f32[1024,3072]{1,0:T(8,128)} %copy-done.34, bf16[1024,768]{1,0:T(8,128)(2,1)} %bitcast.18, bf16[1,3072,768]{2,1,0:T(8,128)(2,1)} %param.28), kind=kOutput, calls=%fused_computation.8 | convolution fusion | flops 4894752768 | bytes 25165824 | tf_op jit(solution)/shard_map/dot_general | solution.py:17
  246.0 8.5 %fusion.41 = bf16[1024,768]{1,0:T(8,128)(2,1)} fusion(bf16[1024,3072]{1,0:T(8,128)(2,1)S(1)} %fusion.6, bf16[1,768,3072]{2,1,0:T(8,128)(2,1)} %param.27), kind=kOutput, calls=%fused_computation.61 | convolution fusion | flops 4832624640 | bytes 12582912 | tf_op jit(solution)/shard_map/dot_general | solution.py:17
  254.5 8.2 %fusion.15 = bf16[1,768,3072]{2,1,0:T(8,128)(2,1)} fusion(bf16[1024,768]{1,0:T(8,128)(2,1)} %bitcast.12, bf16[1024,3072]{1,0:T(8,128)(2,1)S(1)} %fusion.6), kind=kOutput, calls=%fused_computation.25 | convolution fusion | flops 4834197504 | bytes 12582912 | tf_op jit(solution)/shard_map/dot_general | solution.py:17
  262.7 4.2 all-to-all-done.1
  266.9 4.3 all-to-all-start.3
  271.4 12.0 %fusion.16 = bf16[1,3072,768]{2,1,0:T(8,128)(2,1)} fusion(bf16[1024,768]{1,0:T(8,128)(2,1)} %bitcast.18, f32[1024,3072]{1,0:T(8,128)} %copy-done.34), kind=kOutput, calls=%fused_computation.26 | convolution fusion | flops 4862509056 | bytes 18874368 | tf_op jit(solution)/shard_map/dot_general | solution.py:17
  283.5 5.1 multiply_reduce_fusion.2
  288.6 19.1 %all-to-all-done.3 = bf16[8,128,768]{2,1,0:T(8,128)(2,1)} async-done(((bf16[8,128,768]{2,1,0:T(8,128)(2,1)}), bf16[8,128,768]{2,1,0:T(8,128)(2,1)}, u32[]{:S(2)}, u32[]{:S(2)}) %all-to-all-start.3) | async-done | bytes 1572896 | tf_op jit(solution)/shard_map/all_to_all | solution.py:389
  307.7 3.5 fusion.17
  311.2 1.2 multiply_reduce_fusion
  312.6 1.0 copy-done.19
  313.6 1.8 subtract_add_fusion
  315.4 2.6 convolution_convert_fusion.2.grad_ref
  318.0 38.8 %attend_back.1 = (bf16[1024,768]{1,0:T(8,128)(2,1)}, bf16[1024,768]{1,0:T(8,128)(2,1)}, bf16[1024,768]{1,0:T(8,128)(2,1)}, f32[6,4,512]{2,1,0:T(4,128)}) custom-call(bf16[1024,768]{1,0:T(8,128)(2,1)} %copy-done.4, bf16[1024,768]{1,0:T(8,128)(2,1)} %convolution_convert_fusion.4.k_ref, bf16[1024,768]{1,0:T(8,128)(2,1)} %convolution_convert_fusion.3.v_ref, ...), custom_call_target="tpu_custom_call" | custom-call | flops 20132659200 | bytes 12582912 | tf_op jit(solution)/shard_map/attend_back/pallas_call | solution.py:226
  357.6 0.8 slice.102
  359.4 1.2 fusion.90
  361.0 3.3 fusion.88
  364.4 1.4 fusion.89
  366.6 3.7 fusion.34
  370.3 3.0 convolution_convert_fusion.9
  373.3 1.1 constant_dynamic-update-slice_fusion.8
  374.4 1.4 convolution_convert_fusion.8
  375.9 1.1 constant_dynamic-update-slice_fusion.7
  377.0 1.4 convolution_convert_fusion.7
  378.4 1.1 constant_dynamic-update-slice_fusion.6
  380.2 1.4 convolution_convert_fusion.6
  381.7 1.1 constant_dynamic-update-slice_fusion.5
  383.5 1.8 copy.72
  385.4 69.8 %all-reduce.9.cloned.1.call-done = (bf16[1,768,3072]{2,1,0:T(8,128)(2,1)}, bf16[1,3072,768]{2,1,0:T(8,128)(2,1)}) async-done(((bf16[1,768,3072]{2,1,0:T(8,128)(2,1)}, bf16[1,3072,768]{2,1,0:T(8,128)(2,1)}), (bf16[1,768,3072]{2,1,0:T(8,128)(2,1)}, bf16[1,3072,768]{2,1,0:T(8,128)(2,1)})) %all-reduce.9.cloned.1.call-update) | async-done | bytes 9437200 | tf_op jit(solution)/shard_map/psum | solution.py:302
  455.2 101.6 %reduce-scatter.2.cloned.1.call-done = bf16[1,386,768]{2,1,0:T(8,128)(2,1)} async-done(((bf16[8,386,768]{2,1,0:T(8,128)(2,1)}), bf16[1,386,768]{2,1,0:T(8,128)(2,1)}) %reduce-scatter.2.cloned.1.call-update) | async-done | bytes 592912 | tf_op jit(solution)/shard_map/reduce_scatter | solution.py:466
  556.8 3.8 fusion.30
  560.6 1.6 copy.73
  562.2 7.6 %convert_element_type.195 = f32[1,768,3072]{2,1,0:T(8,128)} convert(bf16[1,768,3072]{2,1,0:T(8,128)(2,1)} %get-tuple-element.28) | non-fusion elementwise | flops 2359296 | bytes 14155776 | tf_op jit(solution)/shard_map/convert_element_type | solution.py:487
  569.8 4.5 convert_element_type.196
  574.3 17.2 %all-reduce.7.cloned.1.call-done = bf16[1,386,768]{2,1,0:T(8,128)(2,1)} async-done(((bf16[1,386,768]{2,1,0:T(8,128)(2,1)}), bf16[1,386,768]{2,1,0:T(8,128)(2,1)}) %all-reduce.7.cloned.1.call-update) | async-done | bytes 592912 | tf_op jit(solution)/shard_map/psum | solution.py:302
  592.4 1.1 convert_element_type.194
  593.5 1.0 slice_bitcast_fusion
  (141 shorter events, 13.8 us)
Async XLA Ops:
  7.2 12.0 %copy-start.25 = (s32[1024,1]{0,1:T(1,128)S(1)}, s32[1024,1]{0,1:T(1,128)}, u32[]{:S(2)}) copy-start(s32[1024,1]{0,1:T(1,128)} %param.18) | copy-start | bytes 12292
  7.2 11.1 %copy-start.20 = (bf16[1024,768]{1,0:T(8,128)(2,1)S(1)}, bf16[1024,768]{1,0:T(8,128)(2,1)}, u32[]{:S(2)}) copy-start(bf16[1024,768]{1,0:T(8,128)(2,1)} %param.16) | copy-start | bytes 4718596
  7.2 74.7 %all-gather.4.cloned.1.call-start = ((), (), s32[]{:S(2)}) async-start(), calls=%async_computation.7 | async-start | bytes 5271552 | tf_op jit(solution)/shard_map/all_gather | solution.py:297
  19.1 82.7 %copy-start.6 = (bf16[1024,768]{0,1:T(8,128)(2,1)}, bf16[1024,768]{0,1:T(8,128)(2,1)S(1)}, u32[]{:S(2)}) copy-start(bf16[1024,768]{0,1:T(8,128)(2,1)S(1)} %copy.57) | copy-start | bytes 4718596
  19.6 82.1 %copy-start.26 = (f32[1024]{0:T(1024)}, f32[1024]{0:T(1024)S(1)}, u32[]{:S(2)}) copy-start(f32[1024]{0:T(1024)S(1)} %add_rsqrt_fusion.1) | copy-start | bytes 12292
  90.2 4.7 copy-start.31
  94.4 4.6 copy-start.17
  94.9 6.8 %copy-start.29 = (f32[768]{0:T(1024)}, f32[768]{0:T(1024)S(1)}, u32[]{:S(2)}) copy-start(f32[768]{0:T(1024)S(1)} %reshape.265) | copy-start | bytes 9220
  95.1 8.5 %copy-start.1 = (f32[6,2,512]{2,1,0:T(2,128)}, f32[6,2,512]{2,1,0:T(2,128)S(1)}, u32[]{:S(2)}) copy-start(f32[6,2,512]{2,1,0:T(2,128)S(1)} %copy.61.offset_ref) | copy-start | bytes 73732
  99.0 2.7 copy-start.22
  103.3 34.3 %copy-start.4 = (bf16[1024,768]{1,0:T(8,128)(2,1)}, bf16[1024,768]{1,0:T(8,128)(2,1)S(1)}, u32[]{:S(2)}) copy-start(bf16[1024,768]{1,0:T(8,128)(2,1)S(1)} %convolution_convert_fusion.5.q_ref) | copy-start | bytes 4718596
  103.6 34.1 %copy-start = (bf16[1024,128]{1,0:T(8,128)(2,1)}, bf16[1024,128]{1,0:T(8,128)(2,1)S(1)}, u32[]{:S(2)}) copy-start(bf16[1024,128]{1,0:T(8,128)(2,1)S(1)} %broadcast_in_dim.24.mask_ref) | copy-start | bytes 786436
  103.6 34.1 %copy-start.7 = (bf16[1024,768]{0,1:T(8,128)(2,1)S(1)}, bf16[1024,768]{0,1:T(8,128)(2,1)}, u32[]{:S(2)}) copy-start(bf16[1024,768]{0,1:T(8,128)(2,1)} %copy-done.6) | copy-start | bytes 4718596
  103.6 34.1 %copy-start.23 = (bf16[8,96,768]{2,1,0:T(8,128)(2,1)S(1)}, bf16[8,96,768]{2,1,0:T(8,128)(2,1)}, u32[]{:S(2)}) copy-start(bf16[8,96,768]{2,1,0:T(8,128)(2,1)} %get-tuple-element.72) | copy-start | bytes 3538948
  137.7 1.7 copy-start.2
  137.7 1.7 copy-start.5
  139.4 3.4 copy-start.9
  142.9 42.0 %all-to-all-start = ((bf16[8,128,768]{2,1,0:T(8,128)(2,1)}), bf16[8,128,768]{2,1,0:T(8,128)(2,1)}, u32[]{:S(2)}, u32[]{:S(2)}) async-start(bf16[8,128,768]{2,1,0:T(8,128)(2,1)} %bitcast.11), calls=%async_computation | async-start | bytes 3145728 | tf_op jit(solution)/shard_map/all_to_all | solution.py:389
  149.0 134.5 %copy-start.13 = (bf16[1024,768]{0,1:T(8,128)(2,1)}, bf16[1024,768]{0,1:T(8,128)(2,1)S(1)}, u32[]{:S(2)}) copy-start(bf16[1024,768]{0,1:T(8,128)(2,1)S(1)} %copy.62) | copy-start | bytes 4718596
  184.9 41.0 %all-to-all-start.2 = ((bf16[8,128,768]{2,1,0:T(8,128)(2,1)}), bf16[8,128,768]{2,1,0:T(8,128)(2,1)}, u32[]{:S(2)}, u32[]{:S(2)}) async-start(bf16[8,128,768]{2,1,0:T(8,128)(2,1)} %bitcast.121), calls=%async_computation.2 | async-start | bytes 3145728 | tf_op jit(solution)/shard_map/all_to_all | solution.py:389
  196.6 4.5 copy-start.34
  225.9 41.0 %all-to-all-start.1 = ((bf16[8,128,768]{2,1,0:T(8,128)(2,1)}), bf16[8,128,768]{2,1,0:T(8,128)(2,1)}, u32[]{:S(2)}, u32[]{:S(2)}) async-start(bf16[8,128,768]{2,1,0:T(8,128)(2,1)} %bitcast.120), calls=%async_computation.1 | async-start | bytes 3145728 | tf_op jit(solution)/shard_map/all_to_all | solution.py:389
  266.9 40.8 %all-to-all-start.3 = ((bf16[8,128,768]{2,1,0:T(8,128)(2,1)}), bf16[8,128,768]{2,1,0:T(8,128)(2,1)}, u32[]{:S(2)}, u32[]{:S(2)}) async-start(bf16[8,128,768]{2,1,0:T(8,128)(2,1)} %bitcast.119), calls=%async_computation.3 | async-start | bytes 3145728 | tf_op jit(solution)/shard_map/all_to_all | solution.py:389
  271.2 184.0 %all-reduce.9.cloned.1.call-start = ((), (), s32[]{:S(2)}) async-start(), calls=%async_computation.8 | async-start | bytes 18874368 | tf_op jit(solution)/shard_map/psum | solution.py:302
  283.4 273.3 %reduce-scatter.2.cloned.1.call-start = ((), (), s32[]{:S(2)}) async-start(), calls=%async_computation.5 | async-start | bytes 5419008 | tf_op jit(solution)/shard_map/reduce_scatter | solution.py:466
  307.7 3.5 copy-start.10
  311.2 1.4 copy-start.14
  311.2 2.4 copy-start.19
  313.6 1.8 copy-start.24
  315.4 2.6 copy-start.11
  318.0 42.6 %copy-start.28 = (f32[256,32]{1,0:T(8,128)S(1)}, f32[256,32]{1,0:T(8,128)}, u32[]{:S(2)}) copy-start(f32[256,32]{1,0:T(8,128)} %constant.66) | copy-start | bytes 98308
  361.0 3.3 copy-start.21
  361.0 3.3 copy-start.32
  364.4 1.5 copy-start.8
  364.4 1.9 copy-start.15
  364.4 2.2 copy-start.18
  364.4 2.2 copy-start.27
  364.4 2.2 copy-start.30
  370.3 4.1 copy-start.33
  374.4 2.6 copy-start.16
  377.0 2.6 copy-start.3
  377.0 3.3 copy-start.12
  383.5 208.0 %all-reduce.7.cloned.1.call-start = ((), (), s32[]{:S(2)}) async-start(), calls=%async_computation.6 | async-start | bytes 1204224 | tf_op jit(solution)/shard_map/psum | solution.py:302
  560.6 9.2 %slice-start = ((s8[4718592]{0:T(1024)(128)(4,1)}), s8[524288]{0:T(1024)(128)(4,1)S(1)}, s32[]{:S(2)}) async-start(s8[4718592]{0:T(1024)(128)(4,1)} %bitcast.115), calls=%async_computation.9 | async-start | bytes 1048576
  562.2 7.6 %slice-start.1 = ((s8[4718592]{0:T(1024)(128)(4,1)}), s8[4194304]{0:T(1024)(128)(4,1)S(1)}, s32[]{:S(2)}) async-start(s8[4718592]{0:T(1024)(128)(4,1)} %bitcast.115), calls=%async_computation.10 | async-start | bytes 8388608
Sparse Core Ops, SparseCore 0:
  14.4 67.5 all-gather.3
  283.6 171.5 all-reduce.8
  459.4 97.3 reduce-scatter.1
  559.0 32.5 all-reduce.6

commit v2 on v1

--- a/solution.py
+++ b/solution.py
@@ -331,17 +331,18 @@
             query_weight,
             key_weight,
             value_weight,
-            output_weight,
             pack_small(small_parts, model_width),
         ],
         axis=0,
     )
     whole = gather_packed(packed, group_size)
-    full_query, full_key, full_value, full_output = (
+    whole, later_weight = lax.optimization_barrier((whole, output_weight))
+    full_output = gather_packed(later_weight, group_size).reshape(-1, model_width)
+    full_query, full_key, full_value = (
         whole[:, index * shard_rows : (index + 1) * shard_rows].reshape(-1, model_width)
-        for index in range(4)
-    )
-    small = whole[:, 4 * shard_rows :].reshape(group_size, -1)
+        for index in range(3)
+    )
+    small = whole[:, 3 * shard_rows :].reshape(group_size, -1)
     unpacked = []
     position = 0
     for part in small_parts:
@@ -416,7 +417,8 @@
     active_grad = contract(arrived, weight_out, 1, 1)
     inner_grad = active_pull(active_grad)[0].astype(jnp.bfloat16)
     in_weight_grad = contract(received, inner_grad, 0, 0).astype(jnp.bfloat16)
-    in_total = replica_sum(in_weight_grad[None])
+    in_part = lax.psum_scatter(in_weight_grad[None], "rep", scatter_dimension=1, tiled=True)
+    in_total = lax.all_gather(in_part, "rep", axis=1, tiled=True)
     rows_grad = contract(inner_grad, weight_in, 1, 1).astype(jnp.bfloat16)
     rows_back = exchange(rows_grad)
     combined = contract(dispatch, returned, 0, 0)

time: 613 us -> 617 us (level)
  matrix products: 109 us -> 120 us
  local copies, waits for them, and re-layouts: 44.2 us -> 35.6 us
    psum x2, waiting for transfers between devices: 87 us -> 16.3 us  [replica_sum(): return lax.psum(value, 'rep')]
    all_gather x0 -> x1, waiting for transfers between devices: none -> 38.1 us  [on_device(): in_total = lax.all_gather(in_part, 'rep', axis=1, tiled=True)]
    all_to_all x4, waiting for transfers between devices: 69.3 us -> 103 us  [exchange(): lax.all_to_all(rows.reshape(expert_count, capacity, model_width), 'shard'...]
    reduce_scatter x1, waiting for transfers between devices: 102 us -> 94 us  [on_device(): lax.psum_scatter(grads, 'shard', scatter_dimension=0, tiled=True)]
    unnamed x91 -> x76, local copies, waits for them, and re-layouts: 24.3 us -> 19.8 us
    all_gather x1 -> x2, waiting for transfers between devices: 62.3 us -> 66.4 us  [gather_packed(): whole = lax.all_gather(own, ('shard', 'rep'), axis=0)]
  transfers between devices with their start and end apart: 8 -> 11, of which waited for: 8 -> 9; matrix products, arithmetic and copies ran while one was open for 22% -> 22% of each run, Pallas kernels for 6% -> 12%
where the time goes in v2:
time: 617 us; the launch traced here: 608 us
  waiting for transfers between devices  318 us (52%)
  matrix products  120 us (19%)
  Pallas kernels  73.1 us (12%)
  local copies, waits for them, and re-layouts  35.6 us (6%)
  other arithmetic  27.8 us (5%)
  starting transfers between devices  17.8 us (3%)
  between operations  15.6 us (3%)
    all_to_all x4, waiting for transfers between devices, exchange(): lax.all_to_all(rows.reshape(expert_count, capacity, model_width), 'shard'...  103 us
    reduce_scatter x1, waiting for transfers between devices, on_device(): lax.psum_scatter(grads, 'shard', scatter_dimension=0, tiled=True)  94 us
    dot_general x17, matrix products, contract(): lax.dot_general(left_side, right_side, (((left_axis,), (right_axis,)), ((...  78.7 us
    all_gather x2, waiting for transfers between devices, gather_packed(): whole = lax.all_gather(own, ('shard', 'rep'), axis=0)  66.4 us
    pallas_call x1, Pallas kernels, attend_back(): pl.pallas_call(attend_back_kernel, grid=(pairs,), in_specs=[column, colum...  39.2 us
    all_gather x1, waiting for transfers between devices, on_device(): in_total = lax.all_gather(in_part, 'rep', axis=1, tiled=True)  38.1 us
    pallas_call x1, Pallas kernels, attend(): pl.pallas_call(attend_kernel, grid=(pairs,), in_specs=[column, column, co...  33.9 us
    unnamed x76, local copies, waits for them, and re-layouts  19.8 us
  transfers between devices with their start and end apart: 11, of which 9 were waited for; matrix products, arithmetic and copies ran while one was open for 22% of the time, Pallas kernels for 12%

profile of v2, /device:TPU:0, one launch (start us, length us, event | category | flops | bytes accessed | tf_op | source)
XLA Modules:
  0.0 607.9 jit_solution(17209610346156589181)
XLA Ops:
  7.3 0.8 reshape.232
  8.0 0.8 copy.58
  8.9 0.8 fusion.82
  9.7 1.9 fusion.60
  13.0 2.3 reduce-window.6
  15.7 1.7 copy.57
  17.9 57.7 %all-gather.11.cloned.1.call-done = bf16[32,73,768]{2,1,0:T(8,128)(2,1)} async-done(((bf16[1,73,768]{2,1,0:T(8,128)(2,1)}), bf16[32,73,768]{2,1,0:T(8,128)(2,1)}) %all-gather.11.cloned.1.call-update) | async-done | bytes 3588112 | tf_op jit(solution)/shard_map/all_gather | solution.py:297
  75.6 4.8 reshape.234
  80.4 0.9 slice_bitcast_fusion.4
  82.7 2.2 fusion.92
  84.9 2.7 convolution_convert_fusion.4.k_ref
  87.7 2.8 convolution_convert_fusion.3.v_ref
  90.5 1.6 convolution_convert_fusion.5.q_ref
  92.3 33.9 %attend.1 = (bf16[1024,768]{1,0:T(8,128)(2,1)S(1)}, f32[6,2,1024]{2,1,0:T(2,128)S(1)}) custom-call(bf16[1024,768]{1,0:T(8,128)(2,1)S(1)} %convolution_convert_fusion.5.q_ref, bf16[1024,768]{1,0:T(8,128)(2,1)} %convolution_convert_fusion.4.k_ref, bf16[1024,768]{1,0:T(8,128)(2,1)} %convolution_convert_fusion.3.v_ref, ...), custom_call_target="tpu_custom_call" | custom-call | flops 10066329600 | bytes 6291456 | tf_op jit(solution)/shard_map/attend/pallas_call | solution.py:200
  126.9 8.7 %all-gather.9.cloned.1.call-done = bf16[768,768]{1,0:T(8,128)(2,1)} async-done(((bf16[24,768]{1,0:T(8,128)(2,1)}), bf16[768,768]{1,0:T(8,128)(2,1)}) %all-gather.9.cloned.1.call-update) | async-done | bytes 1179664 | tf_op jit(solution)/shard_map/all_gather | solution.py:297
  135.6 3.4 multiply_reduce_fusion.3
  139.4 3.1 fusion.39
  142.5 4.4 all-to-all-start
  146.9 1.7 copy.62
  149.3 3.2 fusion.40
  152.6 31.9 %all-to-all-done = bf16[8,128,768]{2,1,0:T(8,128)(2,1)} async-done(((bf16[8,128,768]{2,1,0:T(8,128)(2,1)}), bf16[8,128,768]{2,1,0:T(8,128)(2,1)}, u32[]{:S(2)}, u32[]{:S(2)}) %all-to-all-start) | async-done | bytes 1572896 | tf_op jit(solution)/shard_map/all_to_all | solution.py:390
  184.5 4.3 all-to-all-start.2
  188.8 10.5 %fusion.13 = f32[1024,3072]{1,0:T(8,128)} fusion(bf16[1024,768]{1,0:T(8,128)(2,1)} %bitcast.11, bf16[1,768,3072]{2,1,0:T(8,128)(2,1)} %param.27), kind=kOutput, calls=%fused_computation.23 | convolution fusion | flops 4831838208 | bytes 18874368 | tf_op jit(solution)/shard_map/dot_general | solution.py:410
  199.3 26.1 %all-to-all-done.2 = bf16[8,128,768]{2,1,0:T(8,128)(2,1)} async-done(((bf16[8,128,768]{2,1,0:T(8,128)(2,1)}), bf16[8,128,768]{2,1,0:T(8,128)(2,1)}, u32[]{:S(2)}, u32[]{:S(2)}) %all-to-all-start.2) | async-done | bytes 1572896 | tf_op jit(solution)/shard_map/all_to_all | solution.py:390
  225.4 15.3 %fusion.6 = bf16[1024,3072]{1,0:T(8,128)(2,1)S(1)} fusion(f32[1024,3072]{1,0:T(8,128)} %fusion.13, bf16[1024,768]{1,0:T(8,128)(2,1)} %bitcast.17, bf16[1,3072,768]{2,1,0:T(8,128)(2,1)} %param.28), kind=kOutput, calls=%fused_computation.8 | convolution fusion | flops 4894752768 | bytes 25165824 | tf_op jit(solution)/shard_map/dot_general | solution.py:17
  240.8 2.7 copy-done.31
  243.5 8.2 %fusion.15 = bf16[1,768,3072]{2,1,0:T(8,128)(2,1)} fusion(bf16[1024,768]{1,0:T(8,128)(2,1)} %bitcast.11, bf16[1024,3072]{1,0:T(8,128)(2,1)S(1)} %fusion.6), kind=kOutput, calls=%fused_computation.25 | convolution fusion | flops 4834197504 | bytes 12582912 | tf_op jit(solution)/shard_map/dot_general | solution.py:17
  251.7 12.7 %fusion.44 = bf16[1024,768]{1,0:T(8,128)(2,1)} fusion(bf16[1,3072,768]{2,1,0:T(8,128)(2,1)} %param.28, f32[1024,3072]{1,0:T(8,128)} %fusion.13), kind=kOutput, calls=%fused_computation.62 | convolution fusion | flops 4860936192 | bytes 18874368 | tf_op jit(solution)/shard_map/dot_general | solution.py:413
  264.4 4.3 all-to-all-start.1
  268.7 10.3 %fusion.41 = bf16[1024,768]{1,0:T(8,128)(2,1)} fusion(bf16[1024,3072]{1,0:T(8,128)(2,1)} %copy-done.31, bf16[1,768,3072]{2,1,0:T(8,128)(2,1)} %param.27), kind=kOutput, calls=%fused_computation.61 | convolution fusion | flops 4832624640 | bytes 12582912 | tf_op jit(solution)/shard_map/dot_general | solution.py:17
  278.9 26.4 %all-to-all-done.1 = bf16[8,128,768]{2,1,0:T(8,128)(2,1)} async-done(((bf16[8,128,768]{2,1,0:T(8,128)(2,1)}), bf16[8,128,768]{2,1,0:T(8,128)(2,1)}, u32[]{:S(2)}, u32[]{:S(2)}) %all-to-all-start.1) | async-done | bytes 1572896 | tf_op jit(solution)/shard_map/all_to_all | solution.py:390
  305.3 4.3 all-to-all-start.3
  309.7 12.0 %fusion.16 = bf16[1,3072,768]{2,1,0:T(8,128)(2,1)} fusion(bf16[1024,768]{1,0:T(8,128)(2,1)} %bitcast.17, f32[1024,3072]{1,0:T(8,128)} %fusion.13), kind=kOutput, calls=%fused_computation.26 | convolution fusion | flops 4862509056 | bytes 18874368 | tf_op jit(solution)/shard_map/dot_general | solution.py:17
  322.0 5.1 multiply_reduce_fusion.2
  327.6 18.7 %all-to-all-done.3 = bf16[8,128,768]{2,1,0:T(8,128)(2,1)} async-done(((bf16[8,128,768]{2,1,0:T(8,128)(2,1)}), bf16[8,128,768]{2,1,0:T(8,128)(2,1)}, u32[]{:S(2)}, u32[]{:S(2)}) %all-to-all-start.3) | async-done | bytes 1572896 | tf_op jit(solution)/shard_map/all_to_all | solution.py:390
  346.2 3.5 fusion.17
  349.7 1.2 multiply_reduce_fusion
  351.1 1.0 copy-done.21
  352.1 1.8 subtract_add_fusion
  354.0 2.6 convolution_convert_fusion.2.grad_ref
  356.6 39.2 %attend_back.1 = (bf16[1024,768]{1,0:T(8,128)(2,1)}, bf16[1024,768]{1,0:T(8,128)(2,1)}, bf16[1024,768]{1,0:T(8,128)(2,1)}, f32[6,4,512]{2,1,0:T(4,128)}) custom-call(bf16[1024,768]{1,0:T(8,128)(2,1)} %copy-done.6, bf16[1024,768]{1,0:T(8,128)(2,1)} %convolution_convert_fusion.4.k_ref, bf16[1024,768]{1,0:T(8,128)(2,1)} %convolution_convert_fusion.3.v_ref, ...), custom_call_target="tpu_custom_call" | custom-call | flops 20132659200 | bytes 12582912 | tf_op jit(solution)/shard_map/attend_back/pallas_call | solution.py:226
  395.8 0.8 slice.97
  396.6 0.8 slice.96
  397.4 4.0 convolution_convert_fusion.9
  401.4 3.1 fusion.95
  405.1 3.3 fusion.96
  408.7 3.7 fusion.34
  412.9 2.4 constant_dynamic-update-slice_fusion.3
  415.2 3.0 convolution_convert_fusion.8
  418.2 1.1 constant_dynamic-update-slice_fusion.2
  419.3 1.4 convolution_convert_fusion.7
  420.8 1.1 constant_dynamic-update-slice_fusion.1
  421.9 1.4 convolution_convert_fusion.6
  423.3 1.1 constant_dynamic-update-slice_fusion
  425.8 2.1 copy.72
  427.9 94.0 %reduce-scatter.3.cloned.1.call-done = bf16[1,386,768]{2,1,0:T(8,128)(2,1)} async-done(((bf16[8,386,768]{2,1,0:T(8,128)(2,1)}), bf16[1,386,768]{2,1,0:T(8,128)(2,1)}) %reduce-scatter.3.cloned.1.call-update) | async-done | bytes 592912 | tf_op jit(solution)/shard_map/reduce_scatter | solution.py:468
  521.9 38.1 %all-gather.7.cloned.1.call-done = bf16[1,768,3072]{2,1,0:T(8,128)(2,1)} async-done(((bf16[1,192,3072]{2,1,0:T(8,128)(2,1)}), bf16[1,768,3072]{2,1,0:T(8,128)(2,1)}) %all-gather.7.cloned.1.call-update) | async-done | bytes 4718608 | tf_op jit(solution)/shard_map/all_gather | solution.py:421
  560.0 3.8 fusion.30
  563.9 1.6 copy.73
  565.4 7.4 %convert_element_type.195 = f32[1,768,3072]{2,1,0:T(8,128)} convert(bf16[1,768,3072]{2,1,0:T(8,128)(2,1)} %all-gather.7.cloned.1.call-done) | non-fusion elementwise | flops 2359296 | bytes 14155776 | tf_op jit(solution)/shard_map/convert_element_type | solution.py:489
  572.8 6.9 %convert_element_type.196 = f32[1,3072,768]{2,1,0:T(8,128)} convert(bf16[1,3072,768]{2,1,0:T(8,128)(2,1)} %all-reduce.6.cloned.1.call-done) | non-fusion elementwise | flops 2359296 | bytes 14155776 | tf_op jit(solution)/shard_map/convert_element_type | solution.py:490
  579.7 16.3 %all-reduce.8.cloned.1.call-done = bf16[1,386,768]{2,1,0:T(8,128)(2,1)} async-done(((bf16[1,386,768]{2,1,0:T(8,128)(2,1)}), bf16[1,386,768]{2,1,0:T(8,128)(2,1)}) %all-reduce.8.cloned.1.call-update) | async-done | bytes 592912 | tf_op jit(solution)/shard_map/psum | solution.py:302
  596.8 1.1 convert_element_type.194
  598.0 1.0 slice_bitcast_fusion
  (135 shorter events, 11.5 us)
Async XLA Ops:
  7.2 74.8 %copy-start = (bf16[96,768]{1,0:T(8,128)(2,1)S(1)}, bf16[96,768]{1,0:T(8,128)(2,1)}, u32[]{:S(2)}) copy-start(bf16[96,768]{1,0:T(8,128)(2,1)} %param.22) | copy-start | bytes 442372
  7.2 10.3 %copy-start.26 = (s32[1024,1]{0,1:T(1,128)S(1)}, s32[1024,1]{0,1:T(1,128)}, u32[]{:S(2)}) copy-start(s32[1024,1]{0,1:T(1,128)} %param.18) | copy-start | bytes 12292
  7.2 68.4 %all-gather.11.cloned.1.call-start = ((), (), s32[]{:S(2)}) async-start(), calls=%async_computation.12 | async-start | bytes 4055040 | tf_op jit(solution)/shard_map/all_gather | solution.py:297
  11.6 124.0 %all-gather.9.cloned.1.call-start = ((), (), s32[]{:S(2)}) async-start(), calls=%async_computation.11 | async-start | bytes 1216512 | tf_op jit(solution)/shard_map/all_gather | solution.py:297
  17.4 73.1 %copy-start.8 = (bf16[1024,768]{0,1:T(8,128)(2,1)}, bf16[1024,768]{0,1:T(8,128)(2,1)S(1)}, u32[]{:S(2)}) copy-start(bf16[1024,768]{0,1:T(8,128)(2,1)S(1)} %copy.57) | copy-start | bytes 4718596
  17.9 63.9 %copy-start.28 = (bf16[32,512,1]{1,0,2:T(8,128)(2,1)S(1)}, bf16[32,512,1]{1,0,2:T(8,128)(2,1)}, u32[]{:S(2)}) copy-start(bf16[32,512,1]{1,0,2:T(8,128)(2,1)} %constant.71) | copy-start | bytes 98308
  82.0 10.3 %copy-start.3 = (f32[6,2,512]{2,1,0:T(2,128)}, f32[6,2,512]{2,1,0:T(2,128)S(1)}, u32[]{:S(2)}) copy-start(f32[6,2,512]{2,1,0:T(2,128)S(1)} %copy.61.offset_ref) | copy-start | bytes 73732
  84.9 2.8 copy-start.22
  84.9 2.8 copy-start.19
  84.9 5.5 copy-start.23
  92.1 34.2 %copy-start.6 = (bf16[1024,768]{1,0:T(8,128)(2,1)}, bf16[1024,768]{1,0:T(8,128)(2,1)S(1)}, u32[]{:S(2)}) copy-start(bf16[1024,768]{1,0:T(8,128)(2,1)S(1)} %convolution_convert_fusion.5.q_ref) | copy-start | bytes 4718596
  92.3 34.0 %copy-start.2 = (bf16[1024,128]{1,0:T(8,128)(2,1)}, bf16[1024,128]{1,0:T(8,128)(2,1)S(1)}, u32[]{:S(2)}) copy-start(bf16[1024,128]{1,0:T(8,128)(2,1)S(1)} %broadcast_in_dim.24.mask_ref) | copy-start | bytes 786436
  126.3 0.6 copy-start.7
  126.9 12.1 %copy-start.4 = (bf16[1024,768]{1,0:T(8,128)(2,1)}, bf16[1024,768]{1,0:T(8,128)(2,1)S(1)}, u32[]{:S(2)}) copy-start(bf16[1024,768]{1,0:T(8,128)(2,1)S(1)} %get-tuple-element.24.out_ref) | copy-start | bytes 4718596
  139.0 3.4 copy-start.10
  142.5 42.0 %all-to-all-start = ((bf16[8,128,768]{2,1,0:T(8,128)(2,1)}), bf16[8,128,768]{2,1,0:T(8,128)(2,1)}, u32[]{:S(2)}, u32[]{:S(2)}) async-start(bf16[8,128,768]{2,1,0:T(8,128)(2,1)} %bitcast.10), calls=%async_computation | async-start | bytes 3145728 | tf_op jit(solution)/shard_map/all_to_all | solution.py:390
  148.6 173.4 %copy-start.15 = (bf16[1024,768]{0,1:T(8,128)(2,1)}, bf16[1024,768]{0,1:T(8,128)(2,1)S(1)}, u32[]{:S(2)}) copy-start(bf16[1024,768]{0,1:T(8,128)(2,1)S(1)} %copy.62) | copy-start | bytes 4718596
  184.5 41.0 %all-to-all-start.2 = ((bf16[8,128,768]{2,1,0:T(8,128)(2,1)}), bf16[8,128,768]{2,1,0:T(8,128)(2,1)}, u32[]{:S(2)}, u32[]{:S(2)}) async-start(bf16[8,128,768]{2,1,0:T(8,128)(2,1)} %bitcast.120), calls=%async_computation.2 | async-start | bytes 3145728 | tf_op jit(solution)/shard_map/all_to_all | solution.py:390
  188.8 236.4 %reduce-scatter.5.cloned.1.call-start = ((), (), s32[]{:S(2)}) async-start(), calls=%async_computation.7 | async-start | bytes 5898240 | tf_op jit(solution)/shard_map/reduce_scatter | solution.py:420
  240.8 2.7 copy-start.31
  264.4 40.9 %all-to-all-start.1 = ((bf16[8,128,768]{2,1,0:T(8,128)(2,1)}), bf16[8,128,768]{2,1,0:T(8,128)(2,1)}, u32[]{:S(2)}, u32[]{:S(2)}) async-start(bf16[8,128,768]{2,1,0:T(8,128)(2,1)} %bitcast.121), calls=%async_computation.1 | async-start | bytes 3145728 | tf_op jit(solution)/shard_map/all_to_all | solution.py:390
  305.3 40.9 %all-to-all-start.3 = ((bf16[8,128,768]{2,1,0:T(8,128)(2,1)}), bf16[8,128,768]{2,1,0:T(8,128)(2,1)}, u32[]{:S(2)}, u32[]{:S(2)}) async-start(bf16[8,128,768]{2,1,0:T(8,128)(2,1)} %bitcast.119), calls=%async_computation.3 | async-start | bytes 3145728 | tf_op jit(solution)/shard_map/all_to_all | solution.py:390
  309.6 118.3 %all-reduce.6.cloned.1.call-start = ((), (), s32[]{:S(2)}) async-start(), calls=%async_computation.9 | async-start | bytes 9437184 | tf_op jit(solution)/shard_map/psum | solution.py:302
  321.7 200.2 %reduce-scatter.3.cloned.1.call-start = ((), (), s32[]{:S(2)}) async-start(), calls=%async_computation.6 | async-start | bytes 5419008 | tf_op jit(solution)/shard_map/reduce_scatter | solution.py:468
  346.2 3.5 copy-start.11
  349.7 1.4 copy-start.16
  349.7 2.4 copy-start.21
  352.1 1.8 copy-start.29
  354.0 2.6 copy-start.12
  356.6 40.8 %copy-start.9 = (bf16[1024,768]{0,1:T(8,128)(2,1)S(1)}, bf16[1024,768]{0,1:T(8,128)(2,1)}, u32[]{:S(2)}) copy-start(bf16[1024,768]{0,1:T(8,128)(2,1)} %copy-done.8) | copy-start | bytes 4718596
  397.4 4.0 copy-start.24
  397.4 4.0 copy-start.30
  405.0 3.4 copy-start.25
  405.1 3.6 copy-start.14
  405.1 3.6 copy-start.17
  405.1 3.6 copy-start.20
  408.7 3.7 copy-start.27
  415.2 4.1 copy-start.18
  419.3 2.6 copy-start.5
  419.3 2.6 copy-start.13
  425.1 134.9 %all-gather.7.cloned.1.call-start = ((), (), s32[]{:S(2)}) async-start(), calls=%async_computation.8 | async-start | bytes 5898240 | tf_op jit(solution)/shard_map/all_gather | solution.py:421
  425.7 170.3 %all-reduce.8.cloned.1.call-start = ((), (), s32[]{:S(2)}) async-start(), calls=%async_computation.10 | async-start | bytes 1204224 | tf_op jit(solution)/shard_map/psum | solution.py:302
  572.8 28.1 %copy-start.1 = (bf16[96,768]{1,0:T(8,128)(2,1)S(1)}, bf16[96,768]{1,0:T(8,128)(2,1)}, u32[]{:S(2)}) copy-start(bf16[96,768]{1,0:T(8,128)(2,1)} %param.22) | copy-start | bytes 442372
Sparse Core Ops, SparseCore 0:
  11.7 63.8 all-gather.10
  82.8 52.7 all-gather.8
  251.8 47.0 reduce-scatter.4
  321.8 95.4 all-reduce.5
  425.3 96.5 reduce-scatter.2
  523.4 36.5 all-gather.6
  562.5 33.4 all-reduce.7
